TPU v7x, 32 devices: a whole 2x2x4 slice. The times are simulated.
32 devices in a mesh: rep: 2 (over x), shard: 16 (over z, y, core).
Axes of the slice: x: 2, y: 2, z: 4, core: 2. Of those that a mesh axis runs over, the one named last changes fastest.
Arguments:
- tokens: bfloat16 [2, 32, 256, 960], P(None, ('rep', 'shard')), may hold values from -6 to 6
- cotangent: bfloat16 [2, 32, 256, 960], P(None, ('rep', 'shard')), may hold values from -6 to 6
- attn_gain: bfloat16 [960], P('shard'), may hold values from 0.099609375 to 1.8984375
- w_query: bfloat16 [960, 960], P('shard'), may hold values from -0.1875 to 0.1875
- w_key: bfloat16 [960, 320], P('shard'), may hold values from -0.1875 to 0.1875
- w_value: bfloat16 [960, 320], P('shard'), may hold values from -0.1875 to 0.1875
- w_out: bfloat16 [960, 960], P('shard'), may hold values from -0.75 to 0.75
- mlp_gain: bfloat16 [960], P('shard'), may hold values from 0.099609375 to 1.8984375
- w_gate: bfloat16 [960, 2560], P('shard'), may hold values from -0.1875 to 0.1875
- w_up: bfloat16 [960, 2560], P('shard'), may hold values from -0.1875 to 0.1875
- w_down: bfloat16 [2560, 960], P('shard'), may hold values from -0.125 to 0.125
Outputs:
- output: bfloat16 [2, 32, 256, 960], P(None, ('rep', 'shard'))
- grad_tokens: bfloat16 [2, 32, 256, 960], P(None, ('rep', 'shard'))
- grad_attn_gain: float32 [960], P('shard')
- grad_query: float32 [960, 960], P('shard')
- grad_key: float32 [960, 320], P('shard')
- grad_value: float32 [960, 320], P('shard')
- grad_out: float32 [960, 960], P('shard')
- grad_mlp_gain: float32 [960], P('shard')
- grad_gate: float32 [960, 2560], P('shard')
- grad_up: float32 [960, 2560], P('shard')
- grad_down: float32 [2560, 960], P('shard')
All inputs are finite; a program needn't handle non-finite values.
Results may differ from a plain program's by a relative error of at most 0.015.
Values may be sent and summed in bfloat16 or wider, within the bound.
No kernel may reach another device: no remote copies, remote signals or barrier semaphores. Data moves between devices by JAX's collectives and lax.ppermute only.
A program may use at most 192 MiB of HBM per device.

v0:
```python
import functools
import math

import jax
import jax.numpy as jnp
import numpy as np
from jax import lax
from jax.experimental import pallas as pl
from jax.experimental.pallas import tpu as pltpu
from jax.sharding import PartitionSpec as P

HQ = 15
KV = 5
HD = 64
EPSILON = 1e-05
THETA = 100000.0
F32 = jnp.float32
BF16 = jnp.bfloat16
LANES = 128
COLS = 256
NN = ((1,), (0,))
NT = ((1,), (1,))
TN = ((0,), (0,))
VMEM = 60 << 20
ADD_VMEM = 16 << 20


def dot(a, b, contract=NN):
    return lax.dot_general(a, b, (contract, ((), ())), preferred_element_type=F32)


def call(kernel, out_shape, *, vmem=VMEM, **how):
    return pl.pallas_call(
        kernel,
        out_shape=out_shape,
        compiler_params=pltpu.CompilerParams(vmem_limit_bytes=vmem),
        cost_estimate=pl.CostEstimate(flops=1 << 20, bytes_accessed=1 << 12, transcendentals=0),
        **how,
    )


def shape(dims, dtype=BF16):
    return jax.ShapeDtypeStruct(dims, dtype)


def whole(*dims):
    return pl.BlockSpec(dims, lambda *_: (0,) * len(dims))


def once(*dims):
    return pl.BlockSpec(dims, lambda *_: (0,) * len(dims), pipeline_mode=pl.Buffered(1))


def tables(length):
    frequency = THETA ** (-2.0 * np.arange(HD // 2, dtype=np.float32) / HD)
    angles = np.arange(length, dtype=np.float32)[:, None] * frequency.astype(np.float32)[None, :]
    cosine, sine = np.cos(angles), np.sin(angles)
    return np.tile(cosine, (1, 4)), np.concatenate([-sine, sine, -sine, sine], axis=1)


def turn(tile, cosine, sine, low):
    other = jnp.where(low, pltpu.roll(tile, LANES - 32, 1), pltpu.roll(tile, 32, 1))
    return tile * cosine + other * sine


def placed(tile, half):
    lane = lax.broadcasted_iota(jnp.int32, tile.shape, 1)
    alone = jnp.where((lane >= HD) == (half == 1), tile, 0.0)
    moved = pltpu.roll(alone, HD, 1)
    pair = (moved, alone) if half else (alone, moved)
    return [one.astype(BF16) for one in pair]


def attention_forward(x_ref, *refs, wide):
    blocks, (attn_order_ref, mlp_order_ref, plain_order_ref, cos_ref, sin_ref) = refs[:8], refs[8:13]
    two_ref, two_t_ref, keep_ref, send_ref, qkv_ref, probs_ref, mixed_ref, gain_ref, all_ref = refs[13:]

    @pl.when(pl.program_id(0) == 0)
    def _():
        n = all_ref.shape[0] // 16
        for c in range(2):
            near, over_y, over_x, over_both = blocks[4 * c : 4 * c + 4]
            pairs = ((near, over_y), (near, over_x), (over_x, over_both), (over_y, over_both))
            for i, pair in enumerate(pairs):
                for k, ref in enumerate(pair):
                    at = (8 * c + 2 * i + k) * n
                    all_ref[at : at + n, :] = ref[i % 2]

    length, features = x_ref.shape
    half = all_ref.shape[0] // 2
    to_order = attn_order_ref[:, :features]
    last = slice(wide - LANES, wide)
    gains = dot(all_ref[:, last], to_order, TN)
    gain_one, gain_two = gains[HD : HD + 1], gains[HD + 1 : HD + 2]
    gain_ref[...] = gains[HD : HD + 8]
    x = x_ref[...].astype(F32)
    r1 = lax.rsqrt(jnp.mean(x * x, axis=-1, keepdims=True) + EPSILON)
    normed = (x * r1 * gain_one).astype(BF16)
    spread = dot(normed, to_order, NT).astype(BF16)
    turned = dot(to_order, normed, NT).astype(BF16)
    keep_ref[:half, :] = turned[:half]
    send_ref[:half, :] = turned[half:]
    lane = lax.broadcasted_iota(jnp.int32, (length, LANES), 1)
    low = lane % HD < HD // 2
    cosine, sine = cos_ref[...], sin_ref[...]
    tiles, heads = [], {}
    for t in range(wide // LANES):
        cols = slice(t * LANES, (t + 1) * LANES)
        tile = dot(spread, all_ref[:, cols])
        if t * 2 < HQ + KV:
            tile = turn(tile, cosine, sine, low)
        if t == wide // LANES - 1:
            tile = jnp.where(lane < HD, tile, 0.0)
        short = tile.astype(BF16)
        qkv_ref[:, cols] = short
        tiles.append(short)
        for n in (2 * t, 2 * t + 1):
            if HQ <= n < HQ + 2 * KV:
                heads[n] = placed(tile, n % 2)
    causal = lax.broadcasted_iota(jnp.int32, (length, length), 0) >= lax.broadcasted_iota(
        jnp.int32, (length, length), 1
    )
    context = [None] * ((HQ + 1) // 2)
    for h in range(HQ):
        j, t, s = h // (HQ // KV), h // 2, h % 2
        scores = dot(tiles[t], heads[HQ + j][s], NT) * (1.0 / math.sqrt(HD))
        scores = jnp.where(causal, scores, -1e30)
        exponent = jnp.exp(scores - jnp.max(scores, axis=-1, keepdims=True))
        probs = exponent * (1.0 / jnp.sum(exponent, axis=-1, keepdims=True))
        probs = probs.astype(BF16)
        probs_ref[0, h] = probs
        part = dot(probs, heads[HQ + KV + j][s])
        context[t] = part if context[t] is None else context[t] + part
    context = jnp.concatenate([c.astype(BF16) for c in context], axis=1)
    spread = dot(context, attn_order_ref[...], NT).astype(BF16)
    mixed = x + dot(spread, all_ref[:, wide : wide + features])
    spread = dot(attn_order_ref[...], context, NT).astype(BF16)
    keep_ref[half:, :] = spread[:half]
    send_ref[half:, :] = spread[half:]
    mixed_ref[...] = mixed
    r2 = lax.rsqrt(jnp.mean(mixed * mixed, axis=-1, keepdims=True) + EPSILON)
    two = (mixed * r2 * gain_two).astype(BF16)
    two_ref[...] = dot(two, plain_order_ref[:, :features], NT).astype(BF16)
    two_t_ref[...] = dot(mlp_order_ref[:, :features], two, NT).astype(BF16)


def attention_backward(
    mine_ref, other_ref, plain_order_ref, mixed_ref, cot_ref, gain_ref, all_ref, order_ref, qkv_ref,
    probs_ref, cos_ref, sin_ref, x_ref, d_low_ref, d_high_ref, d_attn_ref, out_ref, grad_ref, *, wide
):
    length, features = mixed_ref.shape
    total = (mine_ref[...] + other_ref[...].astype(F32)).astype(BF16)
    d_two = dot(total, plain_order_ref[:, :features])
    mixed = mixed_ref[...]
    r2 = lax.rsqrt(jnp.mean(mixed * mixed, axis=-1, keepdims=True) + EPSILON)
    unit = mixed * r2
    e2 = d_two * gain_ref[1:2, :]
    d_mixed = cot_ref[...].astype(F32) + r2 * (e2 - unit * jnp.mean(e2 * unit, axis=-1, keepdims=True))
    d_attn = d_mixed.astype(BF16)
    d_attn_ref[:, :features] = d_attn
    d_attn_ref[:, features:] = jnp.zeros((length, d_attn_ref.shape[1] - features), BF16)
    grad_gain_two = jnp.sum(d_two * unit, axis=0, keepdims=True)
    d_context = dot(d_attn, all_ref[:, wide : wide + features], NT).astype(BF16)
    d_context = dot(d_context, order_ref[...]).astype(BF16)
    lane = lax.broadcasted_iota(jnp.int32, (length, LANES), 1)
    low = lane % HD < HD // 2
    cosine, sine = cos_ref[...], -sin_ref[...]

    def tile_of(n):
        t = n // 2
        return qkv_ref[:, t * LANES : (t + 1) * LANES]

    d_tiles = [None] * ((HQ + 2 * KV + 1) // 2)

    def add(t, part):
        d_tiles[t] = part if d_tiles[t] is None else d_tiles[t] + part

    groups = HQ // KV
    for j in range(KV):
        keys = placed(tile_of(HQ + j).astype(F32), (HQ + j) % 2)
        values = placed(tile_of(HQ + KV + j).astype(F32), (HQ + KV + j) % 2)
        d_key, d_value = [None, None], [None, None]
        for h in range(j * groups, (j + 1) * groups):
            t, s = h // 2, h % 2
            d_con = d_context[:, t * LANES : (t + 1) * LANES]
            probs = probs_ref[0, h]
            wide_probs = probs.astype(F32)
            d_probs = dot(d_con, values[s], NT)
            inner = jnp.sum(d_probs * wide_probs, axis=-1, keepdims=True)
            d_scores = (wide_probs * (d_probs - inner) * (1.0 / math.sqrt(HD))).astype(BF16)
            add(t, dot(d_scores, keys[s]))
            part = dot(d_scores, tile_of(h), TN)
            d_key[s] = part if d_key[s] is None else d_key[s] + part
            part = dot(probs, d_con, TN)
            d_value[s] = part if d_value[s] is None else d_value[s] + part
        for n, pair in ((HQ + j, d_key), (HQ + KV + j, d_value)):
            here = n % 2
            mask = (lane >= HD) == (here == 1)
            total = jnp.where(mask, pair[here] + pltpu.roll(pair[1 - here], HD, 1), 0.0)
            add(n // 2, total)
    for t, tile in enumerate(d_tiles):
        if t * 2 < HQ + KV:
            tile = turn(tile, cosine, sine, low)
        ref, at = (d_low_ref, t * LANES) if t * LANES < d_low_ref.shape[1] else (d_high_ref, t * LANES - d_low_ref.shape[1])
        ref[:, at : at + LANES] = tile.astype(BF16)
    split = d_low_ref.shape[1]
    d_normed = dot(d_low_ref[...], all_ref[:, :split], NT) + dot(d_high_ref[...], all_ref[:, split:wide], NT)
    d_normed = d_normed.astype(BF16)
    d_normed = dot(d_normed, order_ref[:, :features])
    x = x_ref[...].astype(F32)
    r1 = lax.rsqrt(jnp.mean(x * x, axis=-1, keepdims=True) + EPSILON)
    unit = x * r1
    e1 = d_normed * gain_ref[0:1, :]
    out = d_mixed + r1 * (e1 - unit * jnp.mean(e1 * unit, axis=-1, keepdims=True))
    out_ref[...] = out.astype(BF16)
    grad_gain_one = jnp.sum(d_normed * unit, axis=0, keepdims=True)
    grads = jnp.concatenate([grad_gain_one, grad_gain_two, jnp.zeros((6, features), F32)], axis=0)


    @pl.when(pl.program_id(0) == 0)
    def _():
        grad_ref[...] = grads

    @pl.when(pl.program_id(0) > 0)
    def _():
        grad_ref[...] += grads


def flipped(array, axis, block):
    n = array.shape[axis] // block
    parts = [lax.slice_in_dim(array, i * block, (i + 1) * block, axis=axis) for i in range(n)]
    return jnp.concatenate([parts[i ^ 1] for i in range(n)], axis=axis)


def row_quarters(w, quarter, qr):
    dr, n = w.shape
    parts = []
    for q in range(4):
        part = w[min(q * quarter, dr) : min((q + 1) * quarter, dr), :]
        parts.append(jnp.concatenate([part, jnp.zeros((qr - part.shape[0], n), F32)], axis=0))
    return parts


def pieces_kernel(
    place_ref, wq_ref, wk_ref, wv_ref, wo_ref, g1_ref, g2_ref, wg_ref, wu_ref, wd_ref, attn_ref, mlp_ref,
    *, quarter, qr, pr, fr, wide
):
    rep, dr = place_ref[1], wq_ref.shape[0]

    def store(at, w):
        parts = row_quarters(w, quarter, qr)
        for s in range(2):
            attn_ref[s, :, at : at + w.shape[1]] = jnp.where(rep == 0, parts[s], parts[2 + s]).astype(BF16)

    wide_of = lambda ref: ref[...].astype(F32)
    eye = (
        lax.broadcasted_iota(jnp.int32, (dr, dr), 0) == lax.broadcasted_iota(jnp.int32, (dr, dr), 1)
    ).astype(F32)
    columns = [jnp.sum(eye * wide_of(ref), axis=1, keepdims=True) for ref in (g1_ref, g2_ref)]
    blank = jnp.zeros((dr, wide - wq_ref.shape[1] - 2 * wk_ref.shape[1] - 2), F32)
    store(0, jnp.concatenate([wide_of(wq_ref), wide_of(wk_ref), wide_of(wv_ref)] + columns + [blank], axis=1))
    w = wide_of(wo_ref)
    store(wide, jnp.concatenate([w, jnp.zeros((dr, attn_ref.shape[2] - wide - w.shape[1]), F32)], axis=1))
    halves = []
    for ref in (wg_ref, wu_ref):
        w = wide_of(ref)
        chunks = [w[:, i * fr : (i + 1) * fr] for i in range(w.shape[1] // fr)]
        halves.append([jnp.concatenate(chunks[c::2], axis=1) for c in range(2)])
    row = jnp.concatenate([halves[0][0], halves[1][0], halves[0][1], halves[1][1]], axis=1)
    rows, lanes = pr, mlp_ref.shape[1]
    row = jnp.concatenate([row, jnp.zeros((rows - dr, row.shape[1]), F32)], axis=0).astype(BF16)
    for g in range(4):
        mlp_ref[g * rows : (g + 1) * rows, :] = row[:, g * lanes : (g + 1) * lanes]
    at, n = 4 * rows, wd_ref.shape[1]
    mlp_ref[at : at + fr, :n] = wd_ref[...]
    mlp_ref[at : at + fr, n:] = jnp.zeros((fr, lanes - n), BF16)
    if at + fr < mlp_ref.shape[0]:
        mlp_ref[at + fr :, :] = jnp.zeros((mlp_ref.shape[0] - at - fr, lanes), BF16)


def tie_kernel(*refs):
    del refs


def add_kernel(*refs, n_alpha, count, form):
    totals = [ref[...].astype(F32) for ref in refs[:count]]
    alpha, beta = functools.reduce(jnp.add, totals[:n_alpha]), functools.reduce(jnp.add, totals[n_alpha:])
    if form == "apart":
        refs[-2][:, :, 0] = alpha.astype(BF16)
        refs[-1][:, :, 0] = beta.astype(BF16)
    elif form == "stack":
        refs[-1][0, :, :, 0] = alpha.astype(BF16)
        refs[-1][1, :, :, 0] = beta.astype(BF16)
    else:
        for c in range(alpha.shape[1]):
            refs[-1][c, :, 0] = alpha[:, c].astype(BF16)
            refs[-1][c, :, 1] = beta[:, c].astype(BF16)


def shards_kernel(place_ref, mine_ref, other_ref, got_ref, got_other_ref, gate_ref, up_ref, *, quarter, fr):
    core, rep = place_ref[0], place_ref[1]
    dr = gate_ref.shape[0]
    for at, out_ref in ((0, gate_ref), (1, up_ref)):
        sides = []
        for c, mine, other in ((0, mine_ref, other_ref), (1, got_ref, got_other_ref)):
            a, b = mine[c, at].astype(F32), other[c, at].astype(F32)
            low, high = jnp.where(rep == 0, a, b), jnp.where(rep == 0, b, a)
            rows = [half[s][:quarter] for half in (low, high) for s in range(2)]
            sides.append(jnp.concatenate(rows, axis=0)[:dr])
        even, odd = jnp.where(core == 0, sides[0], sides[1]), jnp.where(core == 0, sides[1], sides[0])
        chunks = []
        for k in range(even.shape[1] // fr):
            chunks += [even[:, k * fr : (k + 1) * fr], odd[:, k * fr : (k + 1) * fr]]
        out_ref[...] = jnp.concatenate(chunks, axis=1)


def attn_shards_kernel(place_ref, mine_ref, other_ref, query_ref, key_ref, value_ref, gains_ref, out_ref, *, quarter, wide):
    rep, dr = place_ref[1], out_ref.shape[0]
    a, b = mine_ref[0, 0].astype(F32), other_ref[0, 0].astype(F32)
    low, high = jnp.where(rep == 0, a, b), jnp.where(rep == 0, b, a)
    rows = jnp.concatenate([half[s][:quarter] for half in (low, high) for s in range(2)], axis=0)[:dr]
    at = 0
    for ref in (query_ref, key_ref, value_ref, gains_ref):
        ref[...] = rows[:, at : at + ref.shape[1]]
        at += ref.shape[1]
    out_ref[...] = rows[:, wide : wide + out_ref.shape[1]]


def order_kernel(*refs):
    for feat_ref, out_ref in zip(refs[:3], refs[3:]):
        column = lax.broadcasted_iota(jnp.int32, out_ref.shape, 1)
        out_ref[...] = (feat_ref[...] == column).astype(F32).astype(BF16)


def copy_kernel(in_ref, *refs):
    out_ref, n = refs[-1], in_ref.shape[1]
    out_ref[:, :n] = in_ref[...]
    out_ref[:, n:] = jnp.zeros((out_ref.shape[0], out_ref.shape[1] - n), BF16)


def sum_kernel(*refs):
    n = refs[-1].shape[1]
    refs[-1][...] = functools.reduce(jnp.add, [r[:, :n].astype(F32) for r in (refs[:3] if len(refs) > 3 else refs[:-1])]).astype(refs[-1].dtype)


def split_attn_kernel(*refs, count):
    rows = refs[0].shape[1]
    for i, ref in enumerate(refs[:count]):
        for s in range(2):
            refs[-1][s, i * rows : (i + 1) * rows, :] = ref[s]


def join_kernel(near_ref, y_ref, x_ref, xy_ref, out_ref):
    rows = near_ref.shape[1]
    blocks = ((near_ref, y_ref), (near_ref, x_ref), (x_ref, xy_ref), (y_ref, xy_ref))
    for i, pair in enumerate(blocks):
        for k, ref in enumerate(pair):
            at = (2 * i + k) * rows
            out_ref[at : at + rows, :] = ref[i % 2]


def attn_grad_kernel(keep_ref, got_ref, *refs, wide, gain_at):
    mine, other = refs[:3], refs[3:6]
    gains_ref, gains_oth_ref, order_ref = refs[6:9]
    out_refs = refs[-4:]
    half, features = keep_ref.shape[0] // 2, gains_ref.shape[1]
    n = out_refs[0].shape[0]
    gains = (gains_ref[...] + gains_oth_ref[...]).astype(BF16)
    gains = dot(order_ref[:half, :features], gains, NT)
    lane = lax.broadcasted_iota(jnp.int32, (half, LANES), 1) + (wide - LANES)
    tile = jnp.where(lane == gain_at, gains[:, 0:1], 0.0) + jnp.where(lane == gain_at + 1, gains[:, 1:2], 0.0)
    column = 0
    for k in range(3):
        at = slice(half, 2 * half) if k == 2 else slice(0, half)
        grad = dot(keep_ref[at, :], mine[k][...]) + dot(got_ref[at, :], other[k][...])
        if k == 1:
            grad = jnp.concatenate([grad[:, :-LANES], grad[:, -LANES:] + tile], axis=1)
        for i, ref in enumerate(out_refs):
            ref[:, column : column + grad.shape[1]] = grad[i * n : (i + 1) * n].astype(BF16)
        column += grad.shape[1]


def mlp_kernel(place_ref, two_ref, two_oth_ref, t_ref, t_oth_ref, cot_ref, cot_oth_ref, w_ref, *refs):
    sends, keeps = refs[:2], refs[2:4]
    down_ref, out_ref, out_oth_ref, d_two_ref, d_two_oth_ref = refs[4:9]
    acts, acts_t, cots, wg, wu, wd, hidden, d_gate, d_up = refs[9:18]
    chunks, down, out, out_oth, d_two, d_two_oth, in_sems, out_sems = refs[18:]
    rows = cot_ref.shape[0]
    width, half_ff, features = acts_t.shape[0], hidden.shape[1], down.shape[1]
    shards, pr = wg.shape[0], wg.shape[1]
    fr, plain, n, block = 2 * half_ff // shards, shards * pr, width // 4, width // 8
    core = place_ref[0]
    started = []

    def fetch(source, target):
        copy = pltpu.make_async_copy(source, target, in_sems.at[len(started)])
        copy.start()
        started.append(copy)
        return copy

    first = [fetch(two_ref, acts.at[pl.ds(0, rows), :])]
    gate_in = fetch(w_ref.at[:, pl.ds(2 * pr * core, pr), :], wg)
    up_in = fetch(w_ref.at[:, pl.ds(2 * pr * core + pr, pr), :], wu)
    cots_in = [fetch(cot_ref, cots.at[pl.ds(0, rows), :])]
    down_in = [
        fetch(
            w_ref.at[2 * k + core, pl.ds(4 * pr, fr), pl.ds(0, wd.shape[1])], wd.at[pl.ds(k * fr, fr), :]
        )
        for k in range(shards // 2)
    ]
    second = [fetch(two_oth_ref, acts.at[pl.ds(rows, rows), :]), fetch(cot_oth_ref, cots.at[pl.ds(rows, rows), :])]
    turned = [fetch(t_ref, acts_t.at[:, pl.ds(0, rows)])]
    for k in range(8):
        source = t_oth_ref.at[pl.ds((k ^ 1) * block, block), :]
        turned.append(fetch(source, acts_t.at[pl.ds(k * block, block), pl.ds(rows, rows)]))

    def wait(copies):
        for copy in copies:
            copy.wait()

    for half in range(2):
        at = slice(half * rows, (half + 1) * rows)
        wait(second if half else first + [gate_in])
        gate = dot(acts[at, :], wg[...].reshape(plain, half_ff))
        if not half:
            wait([up_in])
        up = dot(acts[at, :], wu[...].reshape(plain, half_ff))
        sg = 1.0 / (1.0 + jnp.exp(-gate))
        silu = gate * sg
        hidden[at, :] = (silu * up).astype(BF16)
        if not half:
            wait(cots_in + down_in)
        d_hidden = dot(cots[at, :], wd[...], NT)
        d_gate[at, :] = (d_hidden * up * sg * (1.0 + gate * (1.0 - sg))).astype(BF16)
        d_up[at, :] = (d_hidden * silu).astype(BF16)
    wait(turned)

    going = []

    def put(source, target):
        copy = pltpu.make_async_copy(source, target, out_sems.at[len(going)])
        copy.start()
        going.append(copy)

    for targets, first_row in ((sends, 2 * n), (keeps, 0)):
        for i, d in ((0, d_gate), (1, d_up)):
            grad = dot(acts_t[first_row : first_row + 2 * n, :], d[...])
            for k in range(2):
                slot = len(going) % chunks.shape[0]
                if len(going) >= chunks.shape[0]:
                    going[len(going) - chunks.shape[0]].wait()
                chunks[slot] = grad[k * n : (k + 1) * n].astype(BF16)
                put(chunks.at[slot], targets[k].at[i])
    count = len(going)
    down[...] = dot(hidden[...], cots[:, :features], TN).astype(BF16)
    put(down, down_ref)

    def back(at):
        return dot(d_gate[at, :], wg[...].reshape(plain, half_ff), NT) + dot(
            d_up[at, :], wu[...].reshape(plain, half_ff), NT
        )

    d_two[...] = back(slice(0, rows))
    put(d_two, d_two_ref)
    out[...] = dot(hidden[:rows, :], wd[:, :features])
    put(out, out_ref)
    d_two_oth[...] = back(slice(rows, 2 * rows)).astype(BF16)
    put(d_two_oth, d_two_oth_ref)
    out_oth[...] = dot(hidden[rows:, :], wd[...]).astype(BF16)
    put(out_oth, out_oth_ref)
    wait(going[count - chunks.shape[0] :])


def on_device(
    tokens, cotangent, attn_gain, w_query, w_key, w_value, w_out, mlp_gain, w_gate, w_up, w_down
):
    shards = lax.axis_size("shard")
    chips = shards // 2
    zs = chips // 2
    me, rep = lax.axis_index("shard"), lax.axis_index("rep")
    core = me % 2
    micro, batch, length, features = tokens.shape
    seqs = micro * batch
    rows = seqs * length
    dr = features // shards
    quarter = -(-dr // 4)
    qr = -(-quarter // 8) * 8
    pr = -(-dr // 16) * 16
    plain = shards * pr
    width = shards * 4 * qr
    half = width // 2
    block = zs * qr
    fr = w_down.shape[0]
    half_ff = chips * fr
    nq, nk = HQ * HD, KV * HD
    nqkv = nq + 2 * nk
    wide = -(-(nqkv + 2) // LANES) * LANES
    padded = -(-features // LANES) * LANES
    full = wide + padded
    cosine, sine = (jnp.asarray(t) for t in tables(length))
    place = jnp.stack([core, rep]).astype(jnp.int32)
    in_smem = pl.BlockSpec(memory_space=pltpu.SMEM)
    in_vmem = pl.BlockSpec(memory_space=pltpu.VMEM)
    anywhere = pl.BlockSpec(memory_space=pl.ANY)
    z_bits = zs.bit_length() - 1
    z_flip = np.array([sum(((i >> b) & 1) << (z_bits - 1 - b) for b in range(z_bits)) for i in range(zs)])

    def over(array, flip):
        return lax.ppermute(array, "shard", [(s, s ^ flip) for s in range(shards)])

    def over_core(array):
        return over(array, 1)

    def over_y(array):
        return over(array, 2)

    def over_rep(array):
        return lax.ppermute(array, "rep", [(0, 1), (1, 0)])

    def tie(arrays, *deps):
        return call(
            tie_kernel, [shape(a.shape, a.dtype) for a in arrays],
            in_specs=[anywhere] * (len(arrays) + len(deps)), out_specs=[anywhere] * len(arrays),
            input_output_aliases={i: i for i in range(len(arrays))},
        )(*arrays, *deps)

    def small(kernel, outs, arrays, deps=()):
        return call(
            kernel, outs, in_specs=[in_vmem] * len(arrays) + [anywhere] * len(deps), vmem=16 << 20
        )(*arrays, *deps)

    even = [[2 * k + c for k in range(chips)] for c in range(2)]

    def feature_of(dims):
        sizes = {"core": 2, "split": 2, "f1": 2, "f2": 2, "z": zs, "row": qr}
        grid = np.meshgrid(*[np.arange(sizes[d]) for d in dims], indexing="ij")
        at = {d: g.reshape(-1) for d, g in zip(dims, grid)}
        x_flip = np.where(at["split"] == 0, at["f1"], at["f2"])
        y_flip = np.where(at["split"] == 0, at["f2"], at["f1"])
        shard = me ^ jnp.asarray(at["core"] + 2 * (y_flip + 2 * z_flip[at["z"]]), jnp.int32)
        part = 2 * (rep ^ jnp.asarray(x_flip, jnp.int32)) + jnp.asarray(at["split"], jnp.int32)
        inside = part * quarter + jnp.asarray(at["row"], jnp.int32)
        real = jnp.asarray(at["row"] < quarter) & (inside < dr)
        return jnp.where(real, shard * dr + inside, -1)[:, None]

    feats = [feature_of(("core", "f1", "split", "f2", "z", "row")), feature_of(("f1", "split", "core", "f2", "z", "row"))]
    shard, row = np.repeat(np.arange(shards), pr), np.tile(np.arange(pr), shards)
    feats.append(jnp.asarray(np.where(row < dr, shard * dr + row, -1)[:, None], jnp.int32))
    attn_order, mlp_order, plain_order = call(
        order_kernel, [shape((f.shape[0], padded)) for f in feats], grid=(1,), in_specs=[in_vmem] * 3,
        out_specs=[whole(f.shape[0], padded) for f in feats],
    )(*feats)

    floor = (16 << 20) // (2 * half_ff * shards) + 1
    depth = -(-max(4 * pr + fr, floor) // 16) * 16
    attn_piece, mlp_piece = call(
        functools.partial(pieces_kernel, quarter=quarter, qr=qr, pr=pr, fr=fr, wide=wide),
        [shape((2, qr, full)), shape((depth, half_ff))],
        grid=(1,),
        in_specs=[in_smem] + [
            whole(*w.shape)
            for w in (w_query, w_key, w_value, w_out, attn_gain[None], mlp_gain[None], w_gate, w_up, w_down)
        ],
        out_specs=[in_vmem, whole(depth, half_ff)],
    )(place, w_query, w_key, w_value, w_out, attn_gain[None], mlp_gain[None], w_gate, w_up, w_down)
    mlp = lax.all_gather(mlp_piece, "shard", axis=0, tiled=True).reshape(shards, depth, half_ff)
    parts = [attn_piece if z == 0 else over(attn_piece, 4 * z) for z in z_flip]
    x = tokens.reshape(rows, features)
    cot = cotangent.reshape(rows, features)
    cot_wide = small(copy_kernel, shape((rows, padded)), [cot], [attn_piece])
    cot_oth = over_core(cot_wide)
    attn_near = small(
        functools.partial(split_attn_kernel, count=zs), shape((2, block, full)), parts, [cot_oth, x, attn_order]
    )
    attn_y, attn_x = over_y(attn_near), over_rep(attn_near)
    attn_blocks = [attn_near, attn_y, attn_x, over_rep(attn_y)]
    attn_blocks += [over_core(b) for b in attn_blocks]

    by_rows = lambda cols: pl.BlockSpec((length, cols), lambda i: (i, 0))
    by_cols = lambda n: pl.BlockSpec((n, length), lambda i: (0, i))
    by_once = lambda *arrays: [once(*a.shape) for a in arrays]
    by_probs = pl.BlockSpec((1, HQ, length, length), lambda i: (i, 0, 0, 0))
    rows_at = lambda i, cols: pl.BlockSpec((length, cols), lambda _: (i, 0))
    shared = (*attn_blocks, attn_order, mlp_order, plain_order, cosine, sine)
    two, two_t, keep_t, send_t, qkv, probs, mixed, gain_rows, attn_all = call(
        functools.partial(attention_forward, wide=wide),
        [
            shape((rows, plain)), shape((width, rows)), shape((width, rows)), shape((width, rows)),
            shape((rows, wide)), shape((seqs, HQ, length, length)), shape((rows, features), F32),
            shape((8, features), F32), shape((width, full)),
        ],
        grid=(seqs,),
        in_specs=[by_rows(features)] + by_once(*shared),
        out_specs=[by_rows(plain)] + [by_cols(width)] * 3
        + [by_rows(wide), by_probs, by_rows(features), once(8, features), once(width, full)],
    )(x, *shared)

    n = width // 4
    (
        alpha_send, beta_send, alpha_keep, beta_keep, grad_down, out_part, out_other, d_two_mine, d_two_other
    ) = call(
        mlp_kernel,
        [shape((2, n, half_ff))] * 4 + [shape((half_ff, features))]
        + [shape((rows, features), F32), shape((rows, padded)), shape((rows, plain), F32), shape((rows, plain))],
        in_specs=[in_smem] + [anywhere] * 7,
        out_specs=[anywhere] * 9,
        scratch_shapes=[
            pltpu.VMEM((2 * rows, plain), BF16), pltpu.VMEM((width, 2 * rows), BF16), pltpu.VMEM((2 * rows, padded), BF16),
            pltpu.VMEM((shards, pr, half_ff), BF16), pltpu.VMEM((shards, pr, half_ff), BF16),
            pltpu.VMEM((half_ff, padded), BF16),
            pltpu.VMEM((2 * rows, half_ff), BF16), pltpu.VMEM((2 * rows, half_ff), BF16), pltpu.VMEM((2 * rows, half_ff), BF16),
            pltpu.VMEM((4, n, half_ff), BF16), pltpu.VMEM((half_ff, features), BF16), pltpu.VMEM((rows, features), F32),
            pltpu.VMEM((rows, padded), BF16), pltpu.VMEM((rows, plain), F32), pltpu.VMEM((rows, plain), BF16),
            pltpu.SemaphoreType.DMA((15 + chips,)), pltpu.SemaphoreType.DMA((13,)),
        ],
    )(place, two, over_core(two), two_t, over_core(two_t), cot_wide, cot_oth, mlp)
    grad_down = lax.psum_scatter(
        grad_down, "shard", scatter_dimension=0, tiled=True, axis_index_groups=even
    )

    def add(alpha, beta, at, size, form, deps):
        arrays = [p[0] for p in alpha + beta]
        j, cores, _, _, n = arrays[0].shape
        one = shape((j, cores, 1, size, n))
        outs = {"apart": [one, one], "stack": shape((2,) + one.shape), "last": shape((cores, j, 2, size, n))}[form]
        specs = []
        for _, lead, f in alpha + beta:
            spot = ((0, 0, f, at // size, 0), (j, cores, None, size, n))
            if lead is not None:
                spot = ((lead,) + spot[0], (None,) + spot[1])
            specs.append(pl.BlockSpec(spot[1], functools.partial(lambda where, _: where, spot[0])))
        return call(
            functools.partial(add_kernel, n_alpha=len(alpha), count=len(arrays), form=form), outs, grid=(1,),
            in_specs=specs + [anywhere] * len(deps),
            out_specs=[whole(*o.shape) for o in outs] if form == "apart" else whole(*outs.shape),
            vmem=ADD_VMEM,
        )(*arrays, *deps)

    class Reduction:
        def __init__(self, alpha_keep, beta_keep, alpha_send, beta_send):
            self.early = [[alpha_keep, over_rep(alpha_send)], [beta_keep, over_y(beta_send)]]
            self.late = []
            self.both = []
            self.size = block

        def parts(self, f):
            return [
                [(a, None, f) for a in self.early[s]]
                + [(pair[s], None, 0) for pair in self.late] + [(a, s, 0) for a in self.both]
                for s in range(2)
            ]

        def second(self, *deps):
            alpha_sent, beta_sent = add(*self.parts(1), 0, block, "apart", deps)
            self.late.append((over_y(alpha_sent), over_rep(beta_sent)))
            return [alpha_sent, beta_sent]

        def z(self, *deps):
            self.size //= 2
            sent = add(*self.parts(0), self.size, self.size, "stack", deps)
            self.both.append(over(sent, 4 << (len(self.both))))
            return [sent]

        def last(self, *deps):
            mine = add(*self.parts(0), 0, qr, "last", deps)
            return mine, over_rep(mine)

    mlp_sum = Reduction(
        *[a.reshape(2, 2, 2, block, half_ff) for a in (alpha_keep, beta_keep, alpha_send, beta_send)]
    )

    low = wide // LANES // 8 * 8 * LANES
    arrays = (gain_rows, attn_all, attn_order)
    d_low, d_high, d_attn, grad_tokens, grad_gains = call(
        functools.partial(attention_backward, wide=wide),
        [
            shape((rows, low)), shape((rows, wide - low)), shape((rows, padded)), shape((rows, features)),
            shape((8, features), F32),
        ],
        grid=(seqs,),
        in_specs=[by_rows(plain), by_rows(plain)] + by_once(plain_order) + [by_rows(features)] * 2
        + by_once(*arrays) + [by_rows(wide), by_probs] + by_once(cosine, sine) + [by_rows(features)],
        out_specs=[by_rows(low), by_rows(wide - low), by_rows(padded), by_rows(features), whole(8, features)],
    )(d_two_mine, over_core(d_two_other), plain_order, mixed, cot, *arrays, qkv, probs, cosine, sine, x)
    sent = mlp_sum.second(d_low)
    n = half // 4
    arrays = [d_low, d_high, d_attn]
    arrays = [
        keep_t, over_core(send_t), *arrays, *[over_core(a) for a in arrays], grad_gains, over_core(grad_gains), attn_order
    ]
    attn_grads = call(
        functools.partial(attn_grad_kernel, wide=wide, gain_at=nqkv),
        [shape((n, full))] * 4,
        grid=(1,),
        in_specs=by_once(*arrays) + [anywhere] * 2,
        out_specs=[whole(n, full)] * 4,
        vmem=32 << 20,
    )(*arrays, *sent)
    attn_sum = Reduction(*[a.reshape(1, 1, 2, block, full) for a in attn_grads])
    out_oth = over_core(out_other)
    for i in range(seqs):
        output = call(
            sum_kernel, shape((rows, features)), grid=(1,),
            in_specs=[rows_at(i, features), rows_at(i, features), rows_at(i, padded)]
            + [anywhere] * (2 if i else 1),
            out_specs=rows_at(i, features), input_output_aliases={4: 0} if i else {},
        )(out_part, mixed, out_oth, attn_grads[0], *([output] if i else []))
    sent = mlp_sum.z(attn_grads[0], output)
    sent = attn_sum.second(*sent)
    for step in range(z_bits):
        if step:
            sent = mlp_sum.z(*sent)
        if step == z_bits - 1:
            mlp_mine, mlp_from = None, None
        sent = attn_sum.z(*sent)
    mlp_mine, mlp_from = mlp_sum.last(*sent)
    attn_mine, attn_from = attn_sum.last(mlp_mine)

    grad_gate, grad_up = call(
        functools.partial(shards_kernel, quarter=quarter, fr=fr),
        [shape((dr, 2 * half_ff), F32)] * 2,
        grid=(1,),
        in_specs=[in_smem] + by_once(*[mlp_mine] * 4), out_specs=[whole(dr, 2 * half_ff)] * 2,
    )(place, mlp_mine, mlp_from, over_core(mlp_mine), over_core(mlp_from))
    down_oth = over_rep(grad_down)
    grad_down = call(
        sum_kernel, shape(w_down.shape, F32), grid=(1,), in_specs=[whole(*w_down.shape)] * 2,
        out_specs=whole(*w_down.shape),
    )(grad_down, down_oth)
    grad_query, grad_key, grad_value, grad_gains, grad_out = call(
        functools.partial(attn_shards_kernel, quarter=quarter, wide=wide),
        [shape((dr, n), F32) for n in (nq, nk, nk, 2, features)],
        grid=(1,),
        in_specs=[in_smem] + by_once(attn_mine, attn_mine), out_specs=[whole(dr, n) for n in (nq, nk, nk, 2, features)],
    )(place, attn_mine, attn_from)
    dims = tokens.shape
    return (
        output.reshape(dims), grad_tokens.reshape(dims), grad_gains[:, 0], grad_query, grad_key, grad_value,
        grad_out, grad_gains[:, 1], grad_gate, grad_up, grad_down,
    )


def solution(mesh):
    data = P(None, ("rep", "shard"), None, None)
    vector, matrix = P("shard"), P("shard", None)
    weights = (vector, matrix, matrix, matrix, matrix, vector, matrix, matrix, matrix)
    return jax.shard_map(
        on_device,
        mesh=mesh,
        in_specs=(data, data) + weights,
        out_specs=(data, data) + weights,
        check_vma=False,
    )
```

profile of v0, /device:TPU:0, one launch (start us, length us, event | category | flops | bytes accessed | tf_op | source)
XLA Modules:
  0.0 319.8 jit_solution(367824424966123452)
XLA Ops:
  7.8 2.9 shard_map.311
  12.3 4.7 %collective-permute-start.2 = (bf16[2,16,2688]{2,1,0:T(8,128)(2,1)S(1)}, bf16[2,16,2688]{2,1,0:T(8,128)(2,1)S(1)}, u32[]{:S(2)}, u32[]{:S(2)}) collective-permute-start(bf16[2,16,2688]{2,1,0:T(8,128)(2,1)S(1)} %copy-done.27), channel_id=1, source_target_pairs={{0,12},{1,13},{2,14},{3,15},{4,8},{5,9},{6,10},{7,11},{8,4},{9,5},... | collective-permute-start | bytes 516104 | tf_op jit(solution)/shard_map/ppermute | solution.py:509
  21.2 4.8 %shard_map.313 = (bf16[1024,1024]{1,0:T(8,128)(2,1)}, bf16[1024,1024]{1,0:T(8,128)(2,1)}, bf16[1024,1024]{1,0:T(8,128)(2,1)}) custom-call(s32[1024,1]{1,0:T(8,128)} %copy.42.refs_0_, s32[1024,1]{1,0:T(8,128)} %copy.43.refs_1_, s32[1024,1]{1,0:T(8,128)} %constant.61.clone.refs_2_), custom_call_target="tpu_custom_call" | custom-call | flops 1048576 | bytes 4096 | tf_op jit(solution)/shard_map/pallas_call | solution.py:549
  26.0 4.7 %collective-permute-done.1.refs_2_ = bf16[2,16,2688]{2,1,0:T(8,128)(2,1)} collective-permute-done((bf16[2,16,2688]{2,1,0:T(8,128)(2,1)S(1)}, bf16[2,16,2688]{2,1,0:T(8,128)(2,1)}, u32[]{:S(2)}, u32[]{:S(2)}) %collective-permute-start.1) | collective-permute-done | bytes 172064 | tf_op jit(solution)/shard_map/ppermute | solution.py:509
  30.7 7.3 %collective-permute-done.refs_1_ = bf16[2,16,2688]{2,1,0:T(8,128)(2,1)} collective-permute-done((bf16[2,16,2688]{2,1,0:T(8,128)(2,1)S(1)}, bf16[2,16,2688]{2,1,0:T(8,128)(2,1)}, u32[]{:S(2)}, u32[]{:S(2)}) %collective-permute-start) | collective-permute-done | bytes 172064 | tf_op jit(solution)/shard_map/ppermute | solution.py:509
  38.0 2.0 copy-done.2
  44.2 29.2 %collective-permute-done.4.refs_1_ = bf16[2,64,2688]{2,1,0:T(8,128)(2,1)S(1)} collective-permute-done((bf16[2,64,2688]{2,1,0:T(8,128)(2,1)S(1)}, bf16[2,64,2688]{2,1,0:T(8,128)(2,1)S(1)}, u32[]{:S(2)}, u32[]{:S(2)}) %collective-permute-start.4) | collective-permute-done | bytes 688160 | tf_op jit(solution)/shard_map/ppermute | solution.py:509
  75.5 13.1 %collective-permute-done.6.refs_3_ = bf16[2,64,2688]{2,1,0:T(8,128)(2,1)S(1)} collective-permute-done((bf16[2,64,2688]{2,1,0:T(8,128)(2,1)S(1)}, bf16[2,64,2688]{2,1,0:T(8,128)(2,1)S(1)}, u32[]{:S(2)}, u32[]{:S(2)}) %collective-permute-start.6) | collective-permute-done | bytes 688160 | tf_op jit(solution)/shard_map/ppermute | solution.py:518
  88.6 2.1 collective-permute-done.10.refs_7_
  91.6 30.3 %shard_map.315 = (bf16[512,1024]{1,0:T(8,128)(2,1)}, bf16[1024,512]{1,0:T(8,128)(2,1)}, bf16[1024,512]{1,0:T(8,128)(2,1)}, bf16[1024,512]{1,0:T(8,128)(2,1)}, bf...) custom-call(bf16[512,960]{1,0:T(8,128)(2,1)} %bitcast.32, ...), custom_call_target="tpu_custom_call" | custom-call | flops 1048576 | bytes 4096 | tf_op jit(solution)/shard_map/pallas_call | solution.py:585
  122.4 2.4 collective-permute-done.11.two_oth_ref
  127.3 35.4 %shard_map.316 = (bf16[2,256,1280]{2,1,0:T(8,128)(2,1)}, bf16[2,256,1280]{2,1,0:T(8,128)(2,1)}, bf16[2,256,1280]{2,1,0:T(8,128)(2,1)}, bf16[2,256,1280]{2,1,0:T(...) custom-call(s32[2]{0:T(128)} %pad_add_fusion.place_ref, ...), custom_call_target="tpu_custom_call" | custom-call | flops 1048576 | bytes 4096 | tf_op jit(solution)/shard_map/pallas_call | solution.py:601
  165.7 2.0 collective-permute-start.21
  168.7 25.0 %shard_map.317 = (bf16[512,1024]{1,0:T(8,128)(2,1)}, bf16[512,640]{1,0:T(8,128)(2,1)}, bf16[512,1024]{1,0:T(8,128)(2,1)}, bf16[512,960]{1,0:T(8,128)(2,1)}, f32[8,960]{1,0:T(8,128)}) custom-call(f32[512,1024]{1,0:T(8,128)} %get-tuple-element.66.mine_ref, bf16[512,1024]{1,0:T(8,128)(2,1)} %copy-done.30, ...), custom_call_target="tpu_custom_call" | custom-call | flops 1048576 | bytes 4096 | tf_op jit(solution)/shard_map/pallas_call | solution.py:674
  195.4 12.5 %collective-permute-done.21.refs_3_.refs_4_.refs_5_.refs_6_ = bf16[2,2,2,64,1280]{4,3,2,1,0:T(8,128)(2,1)} collective-permute-done((bf16[2,2,2,64,1280]{4,3,2,1,0:T(8,128)(2,1)}, bf16[2,2,2,64,1280]{4,3,2,1,0:T(8,128)(2,1)}, u32[]{:S(2)}, u32[]{:S(2)}) %collective-permute-start.21) | collective-permute-done | bytes 1310752 | tf_op jit(solution)/shard_map/ppermute | solution.py:509
  209.2 2.7 shard_map.318
  214.3 4.5 %shard_map.319 = (bf16[128,2688]{1,0:T(8,128)(2,1)S(1)}, bf16[128,2688]{1,0:T(8,128)(2,1)S(1)}, bf16[128,2688]{1,0:T(8,128)(2,1)}, bf16[128,2688]{1,0:T(8,128)(2,1)}) custom-call(bf16[1024,512]{1,0:T(8,128)(2,1)S(1)} %copy-done.24, bf16[1024,512]{1,0:T(8,128)(2,1)S(1)} %collective-permute-done.14.got_ref, bf16[512,1024]{1,0:T(8,128)(2,1)S(1)} %copy-done.18, ...), custom_call_target="tpu_custom_call" | custom-call | flops 1048576 | bytes 4096 | tf_op jit(solution)/shard_map/pallas_call | solution.py:691
  222.2 2.6 shard_map.320.refs_4_
  224.9 2.7 shard_map.321.refs_7_
  227.5 2.9 collective-permute-done.24.refs_2_
  234.5 11.1 %collective-permute-done.22.refs_1_ = bf16[1,1,2,64,2688]{4,3,2,1,0:T(8,128)(2,1)} collective-permute-done((bf16[1,1,2,64,2688]{4,3,2,1,0:T(8,128)(2,1)}, bf16[1,1,2,64,2688]{4,3,2,1,0:T(8,128)(2,1)}, u32[]{:S(2)}, u32[]{:S(2)}) %collective-permute-start.22) | collective-permute-done | bytes 688160 | tf_op jit(solution)/shard_map/ppermute | solution.py:518
  245.6 2.0 collective-permute-done.23.refs_3_.refs_4_.refs_5_.refs_6_
  251.2 7.4 %collective-permute-done.26.refs_2_ = bf16[1,1,1,64,2688]{4,3,2,1,0:T(8,128)(2,1)S(1)} collective-permute-done((bf16[1,1,1,64,2688]{4,3,2,1,0:T(8,128)(2,1)S(1)}, bf16[1,1,1,64,2688]{4,3,2,1,0:T(8,128)(2,1)S(1)}, u32[]{:S(2)}, u32[]{:S(2)}) %collective-permute-start.26) | collective-permute-done | bytes 344096 | tf_op jit(solution)/shard_map/ppermute | solution.py:509
  262.9 10.1 %collective-permute-done.28.refs_3_.refs_7_.refs_8_ = bf16[2,1,1,1,32,2688]{5,4,3,2,1,0:T(8,128)(2,1)S(1)} collective-permute-done((bf16[2,1,1,1,32,2688]{5,4,3,2,1,0:T(8,128)(2,1)S(1)}, bf16[2,1,1,1,32,2688]{5,4,3,2,1,0:T(8,128)(2,1)S(1)}, u32[]{:S(2)}, u32[]{:S(2)}) %collective-permute-start.28) | collective-permute-done | bytes 344096 | tf_op jit(solution)/shard_map/ppermute | solution.py:509
  274.2 4.7 %collective-permute-done.31.refs_4_.refs_9_ = bf16[2,2,2,1,16,1280]{5,4,3,2,1,0:T(8,128)(2,1)S(1)} collective-permute-done((bf16[2,2,2,1,16,1280]{5,4,3,2,1,0:T(8,128)(2,1)S(1)}, bf16[2,2,2,1,16,1280]{5,4,3,2,1,0:T(8,128)(2,1)S(1)}, u32[]{:S(2)}, u32[]{:S(2)}) %collective-permute-start.31) | collective-permute-done | bytes 327712 | tf_op jit(solution)/shard_map/ppermute | solution.py:509
  278.9 2.1 shard_map.327.refs_10_.mine_ref
  281.6 7.7 %collective-permute-done.33.other_ref = bf16[2,2,2,16,1280]{4,3,2,1,0:T(8,128)(2,1)} collective-permute-done((bf16[2,2,2,16,1280]{4,3,2,1,0:T(8,128)(2,1)}, bf16[2,2,2,16,1280]{4,3,2,1,0:T(8,128)(2,1)}, u32[]{:S(2)}, u32[]{:S(2)}) %collective-permute-start.33) | collective-permute-done | bytes 327712 | tf_op jit(solution)/shard_map/ppermute | solution.py:518
  296.5 2.2 copy.45
  300.0 3.3 %collective-permute-done.32.other_ref = bf16[1,1,2,16,2688]{4,3,2,1,0:T(8,128)(2,1)S(1)} collective-permute-done((bf16[1,1,2,16,2688]{4,3,2,1,0:T(8,128)(2,1)S(1)}, bf16[1,1,2,16,2688]{4,3,2,1,0:T(8,128)(2,1)S(1)}, u32[]{:S(2)}, u32[]{:S(2)}) %collective-permute-start.32) | collective-permute-done | bytes 172064 | tf_op jit(solution)/shard_map/ppermute | solution.py:518
  304.0 1.9 shard_map.329
  307.4 2.6 shard_map.330
  310.8 2.0 shard_map.331
  (182 shorter events, 54.3 us)
Async XLA Ops:
  7.2 119.1 %all-gather.2.cloned.1.call-start = ((), (), s32[]{:S(2)}) async-start(), calls=%async_computation.1 | async-start | bytes 18104320 | tf_op jit(solution)/shard_map/all_gather | solution.py:566
  10.8 278.5 %reduce-scatter.2.cloned.1.call-start = ((), (), s32[]{:S(2)}) async-start(), calls=%async_computation.2 | async-start | bytes 2949120 | tf_op jit(solution)/shard_map/reduce_scatter | solution.py:617
  11.7 26.2 %collective-permute-start.3 = (bf16[512,1024]{1,0:T(8,128)(2,1)S(1)}, bf16[512,1024]{1,0:T(8,128)(2,1)S(1)}, u32[]{:S(2)}, u32[]{:S(2)}) collective-permute-start(bf16[512,1024]{1,0:T(8,128)(2,1)S(1)} %shard_map.312.cot_ref), channel_id=1, source_target_pairs={{0,1},{1,0},{2,3},{3,2},{4,5},{5,4},{6,7},{7,6},{8,9},{9,8},{10,11... | collective-permute-start | bytes 3145736 | tf_op jit(solution)/shard_map/ppermute | solution.py:509
  12.3 13.8 %collective-permute-start.2 = (bf16[2,16,2688]{2,1,0:T(8,128)(2,1)S(1)}, bf16[2,16,2688]{2,1,0:T(8,128)(2,1)S(1)}, u32[]{:S(2)}, u32[]{:S(2)}) collective-permute-start(bf16[2,16,2688]{2,1,0:T(8,128)(2,1)S(1)} %copy-done.27), channel_id=1, source_target_pairs={{0,12},{1,13},{2,14},{3,15},{4,8},{5,9},{6,10},{7,11},{8,4},{9,5},... | collective-permute-start | bytes 516104 | tf_op jit(solution)/shard_map/ppermute | solution.py:509
  16.9 13.7 %collective-permute-start.1 = (bf16[2,16,2688]{2,1,0:T(8,128)(2,1)S(1)}, bf16[2,16,2688]{2,1,0:T(8,128)(2,1)}, u32[]{:S(2)}, u32[]{:S(2)}) collective-permute-start(bf16[2,16,2688]{2,1,0:T(8,128)(2,1)S(1)} %copy-done.27), channel_id=1, source_target_pairs={{0,4},{1,5},{2,6},{3,7},{4,0},{5,1},{6,2},{7,3},{8,12},{9,13},{10,... | collective-permute-start | bytes 516104 | tf_op jit(solution)/shard_map/ppermute | solution.py:509
  16.9 21.0 %collective-permute-start = (bf16[2,16,2688]{2,1,0:T(8,128)(2,1)S(1)}, bf16[2,16,2688]{2,1,0:T(8,128)(2,1)}, u32[]{:S(2)}, u32[]{:S(2)}) collective-permute-start(bf16[2,16,2688]{2,1,0:T(8,128)(2,1)S(1)} %copy-done.27), channel_id=1, source_target_pairs={{0,8},{1,9},{2,10},{3,11},{4,12},{5,13},{6,14},{7,15},{8,0},{9,1},... | collective-permute-start | bytes 516104 | tf_op jit(solution)/shard_map/ppermute | solution.py:509
  41.1 32.3 %collective-permute-start.4 = (bf16[2,64,2688]{2,1,0:T(8,128)(2,1)S(1)}, bf16[2,64,2688]{2,1,0:T(8,128)(2,1)S(1)}, u32[]{:S(2)}, u32[]{:S(2)}) collective-permute-start(bf16[2,64,2688]{2,1,0:T(8,128)(2,1)S(1)} %shard_map.314.refs_0_), channel_id=1, source_target_pairs={{0,2},{1,3},{2,0},{3,1},{4,6},{5,7},{6,4},{7,5},{8,10},{9,11},{10,... | collective-permute-start | bytes 2064392 | tf_op jit(solution)/shard_map/ppermute | solution.py:509
  42.7 32.7 %collective-permute-start.5 = (bf16[2,64,2688]{2,1,0:T(8,128)(2,1)S(1)}, bf16[2,64,2688]{2,1,0:T(8,128)(2,1)S(1)}, u32[]{:S(2)}, u32[]{:S(2)}) collective-permute-start(bf16[2,64,2688]{2,1,0:T(8,128)(2,1)S(1)} %shard_map.314.refs_0_), channel_id=1, source_target_pairs={{0,16},{16,0},{1,17},{17,1},{2,18},{18,2},{3,19},{19,3},{4,20},{20... | collective-permute-start | bytes 2064392 | tf_op jit(solution)/shard_map/ppermute | solution.py:518
  73.4 15.2 %collective-permute-start.6 = (bf16[2,64,2688]{2,1,0:T(8,128)(2,1)S(1)}, bf16[2,64,2688]{2,1,0:T(8,128)(2,1)S(1)}, u32[]{:S(2)}, u32[]{:S(2)}) collective-permute-start(bf16[2,64,2688]{2,1,0:T(8,128)(2,1)S(1)} %collective-permute-done.4.refs_1_), channel_id=1, source_target_pairs={{0,16},{16,0},{1,17},{17,1},{2,18},{18,2},{3,19},{19,3},{4,20},{20... | collective-permute-start | bytes 2064392 | tf_op jit(solution)/shard_map/ppermute | solution.py:518
  74.9 13.6 %collective-permute-start.7 = (bf16[2,64,2688]{2,1,0:T(8,128)(2,1)S(1)}, bf16[2,64,2688]{2,1,0:T(8,128)(2,1)S(1)}, u32[]{:S(2)}, u32[]{:S(2)}) collective-permute-start(bf16[2,64,2688]{2,1,0:T(8,128)(2,1)S(1)} %shard_map.314.refs_0_), channel_id=1, source_target_pairs={{0,1},{1,0},{2,3},{3,2},{4,5},{5,4},{6,7},{7,6},{8,9},{9,8},{10,11... | collective-permute-start | bytes 2064392 | tf_op jit(solution)/shard_map/ppermute | solution.py:509
  74.9 13.7 %collective-permute-start.8 = (bf16[2,64,2688]{2,1,0:T(8,128)(2,1)S(1)}, bf16[2,64,2688]{2,1,0:T(8,128)(2,1)S(1)}, u32[]{:S(2)}, u32[]{:S(2)}) collective-permute-start(bf16[2,64,2688]{2,1,0:T(8,128)(2,1)S(1)} %collective-permute-done.4.refs_1_), channel_id=1, source_target_pairs={{0,1},{1,0},{2,3},{3,2},{4,5},{5,4},{6,7},{7,6},{8,9},{9,8},{10,11... | collective-permute-start | bytes 2064392 | tf_op jit(solution)/shard_map/ppermute | solution.py:509
  75.4 13.1 %collective-permute-start.9 = (bf16[2,64,2688]{2,1,0:T(8,128)(2,1)S(1)}, bf16[2,64,2688]{2,1,0:T(8,128)(2,1)S(1)}, u32[]{:S(2)}, u32[]{:S(2)}) collective-permute-start(bf16[2,64,2688]{2,1,0:T(8,128)(2,1)S(1)} %collective-permute-done.5.refs_2_), channel_id=1, source_target_pairs={{0,1},{1,0},{2,3},{3,2},{4,5},{5,4},{6,7},{7,6},{8,9},{9,8},{10,11... | collective-permute-start | bytes 2064392 | tf_op jit(solution)/shard_map/ppermute | solution.py:509
  164.1 31.3 %collective-permute-start.20 = (bf16[2,2,2,64,1280]{4,3,2,1,0:T(8,128)(2,1)}, bf16[2,2,2,64,1280]{4,3,2,1,0:T(8,128)(2,1)}, u32[]{:S(2)}, u32[]{:S(2)}) collective-permute-start(bf16[2,2,2,64,1280]{4,3,2,1,0:T(8,128)(2,1)} %bitcast.10), channel_id=1, source_target_pairs={{0,16},{16,0},{1,17},{17,1},{2,18},{18,2},{3,19},{19,3},{4,20},{20... | collective-permute-start | bytes 3932168 | tf_op jit(solution)/shard_map/ppermute | solution.py:518
  165.7 28.6 %collective-permute-start.14 = (bf16[1024,512]{1,0:T(8,128)(2,1)}, bf16[1024,512]{1,0:T(8,128)(2,1)S(1)}, u32[]{:S(2)}, u32[]{:S(2)}) collective-permute-start(bf16[1024,512]{1,0:T(8,128)(2,1)} %get-tuple-element.65), channel_id=1, source_target_pairs={{0,1},{1,0},{2,3},{3,2},{4,5},{5,4},{6,7},{7,6},{8,9},{9,8},{10,11... | collective-permute-start | bytes 3145736 | tf_op jit(solution)/shard_map/ppermute | solution.py:509
  165.7 42.3 %collective-permute-start.21 = (bf16[2,2,2,64,1280]{4,3,2,1,0:T(8,128)(2,1)}, bf16[2,2,2,64,1280]{4,3,2,1,0:T(8,128)(2,1)}, u32[]{:S(2)}, u32[]{:S(2)}) collective-permute-start(bf16[2,2,2,64,1280]{4,3,2,1,0:T(8,128)(2,1)} %bitcast.12), channel_id=1, source_target_pairs={{0,2},{1,3},{2,0},{3,1},{4,6},{5,7},{6,4},{7,5},{8,10},{9,11},{10,... | collective-permute-start | bytes 3932168 | tf_op jit(solution)/shard_map/ppermute | solution.py:509
  193.7 20.6 %collective-permute-start.18 = (bf16[512,1024]{1,0:T(8,128)(2,1)}, bf16[512,1024]{1,0:T(8,128)(2,1)S(1)}, u32[]{:S(2)}, u32[]{:S(2)}) collective-permute-start(bf16[512,1024]{1,0:T(8,128)(2,1)} %get-tuple-element.74.refs_2_), channel_id=1, source_target_pairs={{0,1},{1,0},{2,3},{3,2},{4,5},{5,4},{6,7},{7,6},{8,9},{9,8},{10,11... | collective-permute-start | bytes 3145736 | tf_op jit(solution)/shard_map/ppermute | solution.py:509
  193.9 20.3 %collective-permute-start.16 = (bf16[512,1024]{1,0:T(8,128)(2,1)}, bf16[512,1024]{1,0:T(8,128)(2,1)S(1)}, u32[]{:S(2)}, u32[]{:S(2)}) collective-permute-start(bf16[512,1024]{1,0:T(8,128)(2,1)} %get-tuple-element.72.refs_4_.refs_0_), channel_id=1, source_target_pairs={{0,1},{1,0},{2,3},{3,2},{4,5},{5,4},{6,7},{7,6},{8,9},{9,8},{10,11... | collective-permute-start | bytes 3145736 | tf_op jit(solution)/shard_map/ppermute | solution.py:509
  194.3 19.4 %collective-permute-start.17 = (bf16[512,640]{1,0:T(8,128)(2,1)}, bf16[512,640]{1,0:T(8,128)(2,1)S(1)}, u32[]{:S(2)}, u32[]{:S(2)}) collective-permute-start(bf16[512,640]{1,0:T(8,128)(2,1)} %get-tuple-element.73.refs_1_), channel_id=1, source_target_pairs={{0,1},{1,0},{2,3},{3,2},{4,5},{5,4},{6,7},{7,6},{8,9},{9,8},{10,11... | collective-permute-start | bytes 1966088 | tf_op jit(solution)/shard_map/ppermute | solution.py:509
  195.4 26.8 %collective-permute-start.13 = (bf16[512,1024]{1,0:T(8,128)(2,1)}, bf16[512,1024]{1,0:T(8,128)(2,1)}, u32[]{:S(2)}, u32[]{:S(2)}) collective-permute-start(bf16[512,1024]{1,0:T(8,128)(2,1)} %get-tuple-element.63), channel_id=1, source_target_pairs={{0,1},{1,0},{2,3},{3,2},{4,5},{5,4},{6,7},{7,6},{8,9},{9,8},{10,11... | collective-permute-start | bytes 3145736 | tf_op jit(solution)/shard_map/ppermute | solution.py:509
  211.9 18.5 %collective-permute-start.24 = (bf16[2,2,1,64,1280]{4,3,2,1,0:T(8,128)(2,1)}, bf16[2,2,1,64,1280]{4,3,2,1,0:T(8,128)(2,1)}, u32[]{:S(2)}, u32[]{:S(2)}) collective-permute-start(bf16[2,2,1,64,1280]{4,3,2,1,0:T(8,128)(2,1)} %get-tuple-element.80.refs_9_), channel_id=1, source_target_pairs={{0,2},{1,3},{2,0},{3,1},{4,6},{5,7},{6,4},{7,5},{8,10},{9,11},{10,... | collective-permute-start | bytes 1966088 | tf_op jit(solution)/shard_map/ppermute | solution.py:509
  213.7 17.9 %collective-permute-start.25 = (bf16[2,2,1,64,1280]{4,3,2,1,0:T(8,128)(2,1)}, bf16[2,2,1,64,1280]{4,3,2,1,0:T(8,128)(2,1)}, u32[]{:S(2)}, u32[]{:S(2)}) collective-permute-start(bf16[2,2,1,64,1280]{4,3,2,1,0:T(8,128)(2,1)} %get-tuple-element.81.refs_10_), channel_id=1, source_target_pairs={{0,16},{16,0},{1,17},{17,1},{2,18},{18,2},{3,19},{19,3},{4,20},{20... | collective-permute-start | bytes 1966088 | tf_op jit(solution)/shard_map/ppermute | solution.py:518
  220.5 25.1 %collective-permute-start.22 = (bf16[1,1,2,64,2688]{4,3,2,1,0:T(8,128)(2,1)}, bf16[1,1,2,64,2688]{4,3,2,1,0:T(8,128)(2,1)}, u32[]{:S(2)}, u32[]{:S(2)}) collective-permute-start(bf16[1,1,2,64,2688]{4,3,2,1,0:T(8,128)(2,1)} %bitcast.16), channel_id=1, source_target_pairs={{0,16},{16,0},{1,17},{17,1},{2,18},{18,2},{3,19},{19,3},{4,20},{20... | collective-permute-start | bytes 2064392 | tf_op jit(solution)/shard_map/ppermute | solution.py:518
  222.0 25.7 %collective-permute-start.23 = (bf16[1,1,2,64,2688]{4,3,2,1,0:T(8,128)(2,1)}, bf16[1,1,2,64,2688]{4,3,2,1,0:T(8,128)(2,1)}, u32[]{:S(2)}, u32[]{:S(2)}) collective-permute-start(bf16[1,1,2,64,2688]{4,3,2,1,0:T(8,128)(2,1)} %bitcast.18), channel_id=1, source_target_pairs={{0,2},{1,3},{2,0},{3,1},{4,6},{5,7},{6,4},{7,5},{8,10},{9,11},{10,... | collective-permute-start | bytes 2064392 | tf_op jit(solution)/shard_map/ppermute | solution.py:509
  234.4 27.0 %collective-permute-start.29 = (bf16[2,2,2,1,32,1280]{5,4,3,2,1,0:T(8,128)(2,1)S(1)}, bf16[2,2,2,1,32,1280]{5,4,3,2,1,0:T(8,128)(2,1)S(1)}, u32[]{:S(2)}, u32[]{:S(2)}) collective-permute-start(bf16[2,2,2,1,32,1280]{5,4,3,2,1,0:T(8,128)(2,1)S(1)} %shard_map.322.refs_4_), channel_id=1, source_target_pairs={{0,4},{1,5},{2,6},{3,7},{4,0},{5,1},{6,2},{7,3},{8,12},{9,13},{10,... | collective-permute-start | bytes 1966088 | tf_op jit(solution)/shard_map/ppermute | solution.py:509
  248.9 9.8 %collective-permute-start.26 = (bf16[1,1,1,64,2688]{4,3,2,1,0:T(8,128)(2,1)S(1)}, bf16[1,1,1,64,2688]{4,3,2,1,0:T(8,128)(2,1)S(1)}, u32[]{:S(2)}, u32[]{:S(2)}) collective-permute-start(bf16[1,1,1,64,2688]{4,3,2,1,0:T(8,128)(2,1)S(1)} %get-tuple-element.87.refs_6_), channel_id=1, source_target_pairs={{0,2},{1,3},{2,0},{3,1},{4,6},{5,7},{6,4},{7,5},{8,10},{9,11},{10,... | collective-permute-start | bytes 1032200 | tf_op jit(solution)/shard_map/ppermute | solution.py:509
  250.7 9.4 %collective-permute-start.27 = (bf16[1,1,1,64,2688]{4,3,2,1,0:T(8,128)(2,1)S(1)}, bf16[1,1,1,64,2688]{4,3,2,1,0:T(8,128)(2,1)S(1)}, u32[]{:S(2)}, u32[]{:S(2)}) collective-permute-start(bf16[1,1,1,64,2688]{4,3,2,1,0:T(8,128)(2,1)S(1)} %get-tuple-element.88.refs_7_), channel_id=1, source_target_pairs={{0,16},{16,0},{1,17},{17,1},{2,18},{18,2},{3,19},{19,3},{4,20},{20... | collective-permute-start | bytes 1032200 | tf_op jit(solution)/shard_map/ppermute | solution.py:518
  261.4 11.7 %collective-permute-start.28 = (bf16[2,1,1,1,32,2688]{5,4,3,2,1,0:T(8,128)(2,1)S(1)}, bf16[2,1,1,1,32,2688]{5,4,3,2,1,0:T(8,128)(2,1)S(1)}, u32[]{:S(2)}, u32[]{:S(2)}) collective-permute-start(bf16[2,1,1,1,32,2688]{5,4,3,2,1,0:T(8,128)(2,1)S(1)} %shard_map.324.refs_8_), channel_id=1, source_target_pairs={{0,4},{1,5},{2,6},{3,7},{4,0},{5,1},{6,2},{7,3},{8,12},{9,13},{10,... | collective-permute-start | bytes 1032200 | tf_op jit(solution)/shard_map/ppermute | solution.py:509
  262.8 16.2 %collective-permute-start.31 = (bf16[2,2,2,1,16,1280]{5,4,3,2,1,0:T(8,128)(2,1)S(1)}, bf16[2,2,2,1,16,1280]{5,4,3,2,1,0:T(8,128)(2,1)S(1)}, u32[]{:S(2)}, u32[]{:S(2)}) collective-permute-start(bf16[2,2,2,1,16,1280]{5,4,3,2,1,0:T(8,128)(2,1)S(1)} %shard_map.325.refs_8_), channel_id=1, source_target_pairs={{0,8},{1,9},{2,10},{3,11},{4,12},{5,13},{6,14},{7,15},{8,0},{9,1},... | collective-permute-start | bytes 983048 | tf_op jit(solution)/shard_map/ppermute | solution.py:509
  281.6 25.9 %collective-permute-start.34 = (bf16[2,2,2,16,1280]{4,3,2,1,0:T(8,128)(2,1)}, bf16[2,2,2,16,1280]{4,3,2,1,0:T(8,128)(2,1)}, u32[]{:S(2)}, u32[]{:S(2)}) collective-permute-start(bf16[2,2,2,16,1280]{4,3,2,1,0:T(8,128)(2,1)} %shard_map.327.refs_10_.mine_ref), channel_id=1, source_target_pairs={{0,1},{1,0},{2,3},{3,2},{4,5},{5,4},{6,7},{7,6},{8,9},{9,8},{10,11... | collective-permute-start | bytes 983048 | tf_op jit(solution)/shard_map/ppermute | solution.py:509
  289.3 18.2 %collective-permute-start.35 = (bf16[2,2,2,16,1280]{4,3,2,1,0:T(8,128)(2,1)}, bf16[2,2,2,16,1280]{4,3,2,1,0:T(8,128)(2,1)}, u32[]{:S(2)}, u32[]{:S(2)}) collective-permute-start(bf16[2,2,2,16,1280]{4,3,2,1,0:T(8,128)(2,1)} %collective-permute-done.33.other_ref), channel_id=1, source_target_pairs={{0,1},{1,0},{2,3},{3,2},{4,5},{5,4},{6,7},{7,6},{8,9},{9,8},{10,11... | collective-permute-start | bytes 983048 | tf_op jit(solution)/shard_map/ppermute | solution.py:509
  289.3 20.8 %collective-permute-start.36 = (bf16[160,960]{1,0:T(8,128)(2,1)}, bf16[160,960]{1,0:T(8,128)(2,1)S(1)}, u32[]{:S(2)}, u32[]{:S(2)}) collective-permute-start(bf16[160,960]{1,0:T(8,128)(2,1)} %reduce-scatter.2.cloned.1.call-done.refs_0_), channel_id=1, source_target_pairs={{0,16},{16,0},{1,17},{17,1},{2,18},{18,2},{3,19},{19,3},{4,20},{20... | collective-permute-start | bytes 921608 | tf_op jit(solution)/shard_map/ppermute | solution.py:518
  294.8 8.4 %collective-permute-start.32 = (bf16[1,1,2,16,2688]{4,3,2,1,0:T(8,128)(2,1)S(1)}, bf16[1,1,2,16,2688]{4,3,2,1,0:T(8,128)(2,1)S(1)}, u32[]{:S(2)}, u32[]{:S(2)}) collective-permute-start(bf16[1,1,2,16,2688]{4,3,2,1,0:T(8,128)(2,1)S(1)} %shard_map.328.mine_ref), channel_id=1, source_target_pairs={{0,16},{16,0},{1,17},{17,1},{2,18},{18,2},{3,19},{19,3},{4,20},{20... | collective-permute-start | bytes 516104 | tf_op jit(solution)/shard_map/ppermute | solution.py:518
  (59 other events, 420.9 us)
Sparse Core Ops, SparseCore 0:
  10.8 109.1 all-gather.1
  162.8 84.9 reduce-scatter.1
where the time goes:
time: 324 us; the launch traced here: 320 us
  Pallas kernels  128 us (40%)
  waiting for transfers between devices  126 us (39%)
  starting transfers between devices  25.6 us (8%)
  local copies, waits for them, and re-layouts  25.2 us (8%)
  between operations  14.8 us (5%)
    ppermute x28, waiting for transfers between devices, over(): return lax.ppermute(array, 'shard', [(s, s ^ flip) for s in range(shards)])  86.8 us
    ppermute x9, waiting for transfers between devices, over_rep(): return lax.ppermute(array, 'rep', [(0, 1), (1, 0)])  38.7 us
    pallas_call x1, Pallas kernels, on_device(): call(mlp_kernel, [shape((2, n, half_ff))] * 4 + [shape((half_ff, features...  35.4 us
    pallas_call x1, Pallas kernels, on_device(): call(functools.partial(attention_forward, wide=wide), [shape((rows, plain...  30.3 us
    pallas_call x1, Pallas kernels, on_device(): call(functools.partial(attention_backward, wide=wide), [shape((rows, low)...  25 us
    unnamed x108, local copies, waits for them, and re-layouts  21.6 us
    ppermute x28, starting transfers between devices, over(): return lax.ppermute(array, 'shard', [(s, s ^ flip) for s in range(shards)])  15.8 us
    pallas_call x8, Pallas kernels, add(): call(functools.partial(add_kernel, n_alpha=len(alpha), count=len(arrays),...  12.4 us
  transfers between devices with their start and end apart: 39, of which 19 were waited for; matrix products, arithmetic and copies ran while one was open for 3% of the time, Pallas kernels for 27%

commit v1 on v0

--- a/solution.py
+++ b/solution.py
@@ -314,16 +314,20 @@
         out_ref[...] = jnp.concatenate(chunks, axis=1)
 
 
-def attn_shards_kernel(place_ref, mine_ref, other_ref, query_ref, key_ref, value_ref, gains_ref, out_ref, *, quarter, wide):
+def attn_shards_kernel(place_ref, mine_ref, other_ref, *refs, quarter, wide):
+    query_ref, key_ref, value_ref, *gain_refs, out_ref = refs[-6:]
     rep, dr = place_ref[1], out_ref.shape[0]
     a, b = mine_ref[0, 0].astype(F32), other_ref[0, 0].astype(F32)
     low, high = jnp.where(rep == 0, a, b), jnp.where(rep == 0, b, a)
     rows = jnp.concatenate([half[s][:quarter] for half in (low, high) for s in range(2)], axis=0)[:dr]
     at = 0
-    for ref in (query_ref, key_ref, value_ref, gains_ref):
+    for ref in (query_ref, key_ref, value_ref):
         ref[...] = rows[:, at : at + ref.shape[1]]
         at += ref.shape[1]
     out_ref[...] = rows[:, wide : wide + out_ref.shape[1]]
+    eye = lax.broadcasted_iota(jnp.int32, (dr, dr), 0) == lax.broadcasted_iota(jnp.int32, (dr, dr), 1)
+    for i, ref in enumerate(gain_refs):
+        ref[...] = jnp.sum(jnp.where(eye, rows[:, at + i : at + i + 1], 0.0), axis=0, keepdims=True)
 
 
 def order_kernel(*refs):
@@ -380,11 +384,21 @@
         column += grad.shape[1]
 
 
+def chip_flips(chips):
+    bits = (chips // 2).bit_length() - 1
+    z = [sum(((i >> b) & 1) << (bits - 1 - b) for b in range(bits)) for i in range(chips // 2)]
+    return [2 * flip + y for flip in z for y in range(2)]
+
+
+def fold_kernel(*refs, count):
+    refs[-1][...] = functools.reduce(jnp.add, [r[...].astype(F32) for r in refs[:count]]).astype(refs[-1].dtype)
+
+
 def mlp_kernel(place_ref, two_ref, two_oth_ref, t_ref, t_oth_ref, cot_ref, cot_oth_ref, w_ref, *refs):
     sends, keeps = refs[:2], refs[2:4]
-    down_ref, out_ref, out_oth_ref, d_two_ref, d_two_oth_ref = refs[4:9]
-    acts, acts_t, cots, wg, wu, wd, hidden, d_gate, d_up = refs[9:18]
-    chunks, down, out, out_oth, d_two, d_two_oth, in_sems, out_sems = refs[18:]
+    downs, (out_ref, out_oth_ref, d_two_ref, d_two_oth_ref) = refs[4:6], refs[6:10]
+    acts, acts_t, cots, wg, wu, wd, hidden, d_gate, d_up = refs[10:19]
+    chunks, down, out, out_oth, d_two, d_two_oth, in_sems, out_sems = refs[19:]
     rows = cot_ref.shape[0]
     width, half_ff, features = acts_t.shape[0], hidden.shape[1], down.shape[1]
     shards, pr = wg.shape[0], wg.shape[1]
@@ -453,7 +467,10 @@
                 put(chunks.at[slot], targets[k].at[i])
     count = len(going)
     down[...] = dot(hidden[...], cots[:, :features], TN).astype(BF16)
-    put(down, down_ref)
+    chips = shards // 2
+    for k, flip in enumerate(chip_flips(chips)):
+        source = pl.multiple_of((place_ref[2] ^ flip) * fr, fr)
+        put(down.at[pl.ds(source, fr), :], downs[1 - 2 * k // chips].at[k % (chips // 2)])
 
     def back(at):
         return dot(d_gate[at, :], wg[...].reshape(plain, half_ff), NT) + dot(
@@ -498,7 +515,7 @@
     padded = -(-features // LANES) * LANES
     full = wide + padded
     cosine, sine = (jnp.asarray(t) for t in tables(length))
-    place = jnp.stack([core, rep]).astype(jnp.int32)
+    place = jnp.stack([core, rep, me // 2]).astype(jnp.int32)
     in_smem = pl.BlockSpec(memory_space=pltpu.SMEM)
     in_vmem = pl.BlockSpec(memory_space=pltpu.VMEM)
     anywhere = pl.BlockSpec(memory_space=pl.ANY)
@@ -529,7 +546,6 @@
             kernel, outs, in_specs=[in_vmem] * len(arrays) + [anywhere] * len(deps), vmem=16 << 20
         )(*arrays, *deps)
 
-    even = [[2 * k + c for k in range(chips)] for c in range(2)]
 
     def feature_of(dims):
         sizes = {"core": 2, "split": 2, "f1": 2, "f2": 2, "z": zs, "row": qr}
@@ -597,13 +613,14 @@
 
     n = width // 4
     (
-        alpha_send, beta_send, alpha_keep, beta_keep, grad_down, out_part, out_other, d_two_mine, d_two_other
+        alpha_send, beta_send, alpha_keep, beta_keep, down_send, down_keep, out_part, out_other, d_two_mine,
+        d_two_other,
     ) = call(
         mlp_kernel,
-        [shape((2, n, half_ff))] * 4 + [shape((half_ff, features))]
+        [shape((2, n, half_ff))] * 4 + [shape((chips // 2, fr, features))] * 2
         + [shape((rows, features), F32), shape((rows, padded)), shape((rows, plain), F32), shape((rows, plain))],
         in_specs=[in_smem] + [anywhere] * 7,
-        out_specs=[anywhere] * 9,
+        out_specs=[anywhere] * 10,
         scratch_shapes=[
             pltpu.VMEM((2 * rows, plain), BF16), pltpu.VMEM((width, 2 * rows), BF16), pltpu.VMEM((2 * rows, padded), BF16),
             pltpu.VMEM((shards, pr, half_ff), BF16), pltpu.VMEM((shards, pr, half_ff), BF16),
@@ -611,12 +628,28 @@
             pltpu.VMEM((2 * rows, half_ff), BF16), pltpu.VMEM((2 * rows, half_ff), BF16), pltpu.VMEM((2 * rows, half_ff), BF16),
             pltpu.VMEM((4, n, half_ff), BF16), pltpu.VMEM((half_ff, features), BF16), pltpu.VMEM((rows, features), F32),
             pltpu.VMEM((rows, padded), BF16), pltpu.VMEM((rows, plain), F32), pltpu.VMEM((rows, plain), BF16),
-            pltpu.SemaphoreType.DMA((15 + chips,)), pltpu.SemaphoreType.DMA((13,)),
+            pltpu.SemaphoreType.DMA((15 + chips,)), pltpu.SemaphoreType.DMA((12 + chips,)),
         ],
     )(place, two, over_core(two), two_t, over_core(two_t), cot_wide, cot_oth, mlp)
-    grad_down = lax.psum_scatter(
-        grad_down, "shard", scatter_dimension=0, tiled=True, axis_index_groups=even
-    )
+    def fold(parts, n, at, deps=()):
+        spec = pl.BlockSpec((n, fr, features), lambda _: (at, 0, 0))
+        return call(
+            functools.partial(fold_kernel, count=len(parts)), shape((n, fr, features)), grid=(1,),
+            in_specs=[spec] * len(parts) + [anywhere] * len(deps), out_specs=whole(n, fr, features), vmem=ADD_VMEM,
+        )(*parts, *deps)
+
+    down_parts = [down_keep, over(down_send, 4)]
+
+    def down_stages():
+        n = chips // 2
+        for flip in [4 << b for b in range(1, z_bits)] + [2]:
+            n //= 2
+            yield n, flip
+
+    def down_stage(n, flip, *deps):
+        sent = fold(down_parts, n, 1, deps)
+        down_parts.append(over(sent, flip))
+        return [sent]
 
     def add(alpha, beta, at, size, form, deps):
         arrays = [p[0] for p in alpha + beta]
@@ -681,23 +714,26 @@
         in_specs=[by_rows(plain), by_rows(plain)] + by_once(plain_order) + [by_rows(features)] * 2
         + by_once(*arrays) + [by_rows(wide), by_probs] + by_once(cosine, sine) + [by_rows(features)],
         out_specs=[by_rows(low), by_rows(wide - low), by_rows(padded), by_rows(features), whole(8, features)],
+        vmem=40 << 20,
     )(d_two_mine, over_core(d_two_other), plain_order, mixed, cot, *arrays, qkv, probs, cosine, sine, x)
-    sent = mlp_sum.second(d_low)
+    down_left = list(down_stages())
+    out_oth, got_t = over_core(out_other), over_core(send_t)
+    sent = down_stage(*down_left.pop(0), d_low, out_oth, got_t)
+    sent += mlp_sum.second(*sent)
     n = half // 4
     arrays = [d_low, d_high, d_attn]
     arrays = [
-        keep_t, over_core(send_t), *arrays, *[over_core(a) for a in arrays], grad_gains, over_core(grad_gains), attn_order
+        keep_t, got_t, *arrays, *[over_core(a) for a in arrays], grad_gains, over_core(grad_gains), attn_order
     ]
     attn_grads = call(
         functools.partial(attn_grad_kernel, wide=wide, gain_at=nqkv),
         [shape((n, full))] * 4,
         grid=(1,),
-        in_specs=by_once(*arrays) + [anywhere] * 2,
+        in_specs=by_once(*arrays) + [anywhere] * len(sent),
         out_specs=[whole(n, full)] * 4,
         vmem=32 << 20,
     )(*arrays, *sent)
     attn_sum = Reduction(*[a.reshape(1, 1, 2, block, full) for a in attn_grads])
-    out_oth = over_core(out_other)
     for i in range(seqs):
         output = call(
             sum_kernel, shape((rows, features)), grid=(1,),
@@ -710,10 +746,14 @@
     for step in range(z_bits):
         if step:
             sent = mlp_sum.z(*sent)
-        if step == z_bits - 1:
-            mlp_mine, mlp_from = None, None
+        if down_left:
+            sent = down_stage(*down_left.pop(0), *sent)
         sent = attn_sum.z(*sent)
-    mlp_mine, mlp_from = mlp_sum.last(*sent)
+    while down_left:
+        sent = down_stage(*down_left.pop(0), *sent)
+    down_mine = fold(down_parts, 1, 0, sent)
+    down_from = over_rep(down_mine)
+    mlp_mine, mlp_from = mlp_sum.last(down_mine)
     attn_mine, attn_from = attn_sum.last(mlp_mine)
 
     grad_gate, grad_up = call(
@@ -722,21 +762,22 @@
         grid=(1,),
         in_specs=[in_smem] + by_once(*[mlp_mine] * 4), out_specs=[whole(dr, 2 * half_ff)] * 2,
     )(place, mlp_mine, mlp_from, over_core(mlp_mine), over_core(mlp_from))
-    down_oth = over_rep(grad_down)
     grad_down = call(
-        sum_kernel, shape(w_down.shape, F32), grid=(1,), in_specs=[whole(*w_down.shape)] * 2,
-        out_specs=whole(*w_down.shape),
-    )(grad_down, down_oth)
-    grad_query, grad_key, grad_value, grad_gains, grad_out = call(
+        functools.partial(fold_kernel, count=2), shape((1, fr, features), F32), grid=(1,),
+        in_specs=by_once(down_mine, down_mine) + [anywhere], out_specs=whole(1, fr, features), vmem=ADD_VMEM,
+    )(down_mine, down_from, grad_gate)
+    attn_dims = ((dr, nq), (dr, nk), (dr, nk), (1, dr), (1, dr), (dr, features))
+    grad_query, grad_key, grad_value, grad_gain_one, grad_gain_two, grad_out = call(
         functools.partial(attn_shards_kernel, quarter=quarter, wide=wide),
-        [shape((dr, n), F32) for n in (nq, nk, nk, 2, features)],
+        [shape(dims, F32) for dims in attn_dims],
         grid=(1,),
-        in_specs=[in_smem] + by_once(attn_mine, attn_mine), out_specs=[whole(dr, n) for n in (nq, nk, nk, 2, features)],
-    )(place, attn_mine, attn_from)
+        in_specs=[in_smem] + by_once(attn_mine, attn_mine) + [anywhere] * 2,
+        out_specs=[whole(*dims) for dims in attn_dims],
+    )(place, attn_mine, attn_from, grad_down, grad_gate)
     dims = tokens.shape
     return (
-        output.reshape(dims), grad_tokens.reshape(dims), grad_gains[:, 0], grad_query, grad_key, grad_value,
-        grad_out, grad_gains[:, 1], grad_gate, grad_up, grad_down,
+        output.reshape(dims), grad_tokens.reshape(dims), grad_gain_one.reshape(dr), grad_query, grad_key, grad_value,
+        grad_out, grad_gain_two.reshape(dr), grad_gate, grad_up, grad_down[0],
     )
 
 

time: 324 us -> 307 us (0.948)
  waiting for transfers between devices: 126 us -> 111 us
  Pallas kernels: 128 us -> 123 us
  starting transfers between devices: 25.6 us -> 30.1 us
    ppermute x9, waiting for transfers between devices: 38.7 us -> 29.8 us  [over_rep(): return lax.ppermute(array, 'rep', [(0, 1), (1, 0)])]
    ppermute x28 -> x31, waiting for transfers between devices: 86.8 us -> 81.2 us  [over(): return lax.ppermute(array, 'shard', [(s, s ^ flip) for s in range(shards)])]
    pallas_call x1, Pallas kernels: 25 us -> 21 us  [on_device(): call(functools.partial(attention_backward, wide=wide), [shape((rows, low)...]
    ppermute x28 -> x31, starting transfers between devices: 15.8 us -> 18.4 us  [over(): return lax.ppermute(array, 'shard', [(s, s ^ flip) for s in range(shards)])]
    unnamed x108 -> x118, local copies, waits for them, and re-layouts: 21.6 us -> 20.3 us
    pallas_call x2 -> x5, Pallas kernels: 37.4 us -> 38.2 us  [the longest x1 35.2 us: on_device(): call(mlp_kernel, [shape((2, n, half_ff))] * 4 + [shape((chips // 2, fr, f...]
  transfers between devices with their start and end apart: 39 -> 41, of which waited for: 19 -> 20; matrix products, arithmetic and copies ran while one was open for 3% -> 2% of each run, Pallas kernels for 27% -> 27%
where the time goes in v1:
time: 307 us; the launch traced here: 303 us
  Pallas kernels  123 us (40%)
  waiting for transfers between devices  111 us (36%)
  starting transfers between devices  30.1 us (10%)
  local copies, waits for them, and re-layouts  22.3 us (7%)
  between operations  14.9 us (5%)
    ppermute x31, waiting for transfers between devices, over(): return lax.ppermute(array, 'shard', [(s, s ^ flip) for s in range(shards)])  81.2 us
    pallas_call x1, Pallas kernels, on_device(): call(mlp_kernel, [shape((2, n, half_ff))] * 4 + [shape((chips // 2, fr, f...  35.2 us
    pallas_call x1, Pallas kernels, on_device(): call(functools.partial(attention_forward, wide=wide), [shape((rows, plain...  30.6 us
    ppermute x9, waiting for transfers between devices, over_rep(): return lax.ppermute(array, 'rep', [(0, 1), (1, 0)])  29.8 us
    pallas_call x1, Pallas kernels, on_device(): call(functools.partial(attention_backward, wide=wide), [shape((rows, low)...  21 us
    unnamed x118, local copies, waits for them, and re-layouts  20.3 us
    ppermute x31, starting transfers between devices, over(): return lax.ppermute(array, 'shard', [(s, s ^ flip) for s in range(shards)])  18.4 us
    ppermute x9, starting transfers between devices, over_rep(): return lax.ppermute(array, 'rep', [(0, 1), (1, 0)])  11.7 us
  transfers between devices with their start and end apart: 41, of which 20 were waited for; matrix products, arithmetic and copies ran while one was open for 2% of the time, Pallas kernels for 27%

profile of v1, /device:TPU:0, one launch (start us, length us, event | category | flops | bytes accessed | tf_op | source)
XLA Modules:
  0.0 302.5 jit_solution(851610132334973624)
XLA Ops:
  7.9 2.8 shard_map.311
  12.3 4.7 %collective-permute-start.2 = (bf16[2,16,2688]{2,1,0:T(8,128)(2,1)S(1)}, bf16[2,16,2688]{2,1,0:T(8,128)(2,1)S(1)}, u32[]{:S(2)}, u32[]{:S(2)}) collective-permute-start(bf16[2,16,2688]{2,1,0:T(8,128)(2,1)S(1)} %copy-done.35), channel_id=1, source_target_pairs={{0,12},{1,13},{2,14},{3,15},{4,8},{5,9},{6,10},{7,11},{8,4},{9,5},... | collective-permute-start | bytes 516104 | tf_op jit(solution)/shard_map/ppermute | solution.py:526
  21.3 4.8 %shard_map.313 = (bf16[1024,1024]{1,0:T(8,128)(2,1)}, bf16[1024,1024]{1,0:T(8,128)(2,1)}, bf16[1024,1024]{1,0:T(8,128)(2,1)}) custom-call(s32[1024,1]{1,0:T(8,128)} %copy.42.refs_0_, s32[1024,1]{1,0:T(8,128)} %copy.43.refs_1_, s32[1024,1]{1,0:T(8,128)} %constant.71.clone.refs_2_), custom_call_target="tpu_custom_call" | custom-call | flops 1048576 | bytes 4096 | tf_op jit(solution)/shard_map/pallas_call | solution.py:565
  26.1 4.7 %collective-permute-done.1.refs_2_ = bf16[2,16,2688]{2,1,0:T(8,128)(2,1)} collective-permute-done((bf16[2,16,2688]{2,1,0:T(8,128)(2,1)S(1)}, bf16[2,16,2688]{2,1,0:T(8,128)(2,1)}, u32[]{:S(2)}, u32[]{:S(2)}) %collective-permute-start.1) | collective-permute-done | bytes 172064 | tf_op jit(solution)/shard_map/ppermute | solution.py:526
  30.7 7.3 %collective-permute-done.refs_1_ = bf16[2,16,2688]{2,1,0:T(8,128)(2,1)} collective-permute-done((bf16[2,16,2688]{2,1,0:T(8,128)(2,1)S(1)}, bf16[2,16,2688]{2,1,0:T(8,128)(2,1)}, u32[]{:S(2)}, u32[]{:S(2)}) %collective-permute-start) | collective-permute-done | bytes 172064 | tf_op jit(solution)/shard_map/ppermute | solution.py:526
  38.1 1.7 copy-done.2
  40.9 1.6 collective-permute-start.4
  44.0 29.1 %collective-permute-done.4.refs_1_ = bf16[2,64,2688]{2,1,0:T(8,128)(2,1)S(1)} collective-permute-done((bf16[2,64,2688]{2,1,0:T(8,128)(2,1)S(1)}, bf16[2,64,2688]{2,1,0:T(8,128)(2,1)S(1)}, u32[]{:S(2)}, u32[]{:S(2)}) %collective-permute-start.4) | collective-permute-done | bytes 688160 | tf_op jit(solution)/shard_map/ppermute | solution.py:526
  75.2 12.9 %collective-permute-done.6.refs_3_ = bf16[2,64,2688]{2,1,0:T(8,128)(2,1)S(1)} collective-permute-done((bf16[2,64,2688]{2,1,0:T(8,128)(2,1)S(1)}, bf16[2,64,2688]{2,1,0:T(8,128)(2,1)S(1)}, u32[]{:S(2)}, u32[]{:S(2)}) %collective-permute-start.6) | collective-permute-done | bytes 688160 | tf_op jit(solution)/shard_map/ppermute | solution.py:535
  88.2 2.1 collective-permute-done.10.refs_7_
  91.2 30.6 %shard_map.315 = (bf16[512,1024]{1,0:T(8,128)(2,1)}, bf16[1024,512]{1,0:T(8,128)(2,1)}, bf16[1024,512]{1,0:T(8,128)(2,1)}, bf16[1024,512]{1,0:T(8,128)(2,1)}, bf...) custom-call(bf16[512,960]{1,0:T(8,128)(2,1)} %bitcast.36, ...), custom_call_target="tpu_custom_call" | custom-call | flops 1048576 | bytes 4096 | tf_op jit(solution)/shard_map/pallas_call | solution.py:601
  122.3 2.8 collective-permute-done.11.two_oth_ref
  126.4 35.2 %shard_map.316 = (bf16[2,256,1280]{2,1,0:T(8,128)(2,1)}, bf16[2,256,1280]{2,1,0:T(8,128)(2,1)}, bf16[2,256,1280]{2,1,0:T(8,128)(2,1)}, bf16[2,256,1280]{2,1,0:T(...) custom-call(s32[3]{0:T(128)} %pad_add_fusion.place_ref, ...), custom_call_target="tpu_custom_call" | custom-call | flops 1048576 | bytes 4096 | tf_op jit(solution)/shard_map/pallas_call | solution.py:618
  164.5 1.8 collective-permute-start.22
  167.9 1.6 copy-done.29
  171.0 21.0 %shard_map.317 = (bf16[512,1024]{1,0:T(8,128)(2,1)S(1)}, bf16[512,640]{1,0:T(8,128)(2,1)S(1)}, bf16[512,1024]{1,0:T(8,128)(2,1)S(1)}, bf16[512,960]{1,0:T(8,128)(2,1)S(1)}, f32[8,960]{1,0:T(8,128)S(1)}) custom-call(f32[512,1024]{1,0:T(8,128)S(1)} %copy-done.29, bf16[512,1024]{1,0:T(8,128)(2,1)S(1)} %collective-permute-done.15.other_ref, ...), custom_call_target="tpu_custom_call" | custom-call | flops 1048576 | bytes 4096 | tf_op jit(solution)/shard_map/pallas_call | solution.py:707
  197.7 1.9 collective-permute-start.25
  201.1 4.5 %shard_map.320 = (bf16[128,2688]{1,0:T(8,128)(2,1)S(1)}, bf16[128,2688]{1,0:T(8,128)(2,1)S(1)}, bf16[128,2688]{1,0:T(8,128)(2,1)}, bf16[128,2688]{1,0:T(8,128)(2,1)}) custom-call(bf16[1024,512]{1,0:T(8,128)(2,1)S(1)} %copy-done.31, bf16[1024,512]{1,0:T(8,128)(2,1)S(1)} %copy-done.25, bf16[512,1024]{1,0:T(8,128)(2,1)S(1)} %get-tuple-element.74.refs_2_.refs_0_, ...), custom_call_target="tpu_custom_call" | custom-call | flops 1048576 | bytes 4096 | tf_op jit(solution)/shard_map/pallas_call | solution.py:728
  207.7 2.6 shard_map.321.refs_4_
  210.3 2.7 shard_map.322.refs_7_
  213.0 2.6 collective-permute-done.25.refs_2_
  215.6 1.8 collective-permute-done.26.refs_5_.refs_6_.refs_7_
  222.7 1.9 collective-permute-start.31
  224.6 6.9 %collective-permute-done.23.refs_1_ = bf16[1,1,2,64,2688]{4,3,2,1,0:T(8,128)(2,1)} collective-permute-done((bf16[1,1,2,64,2688]{4,3,2,1,0:T(8,128)(2,1)}, bf16[1,1,2,64,2688]{4,3,2,1,0:T(8,128)(2,1)}, u32[]{:S(2)}, u32[]{:S(2)}) %collective-permute-start.23) | collective-permute-done | bytes 688160 | tf_op jit(solution)/shard_map/ppermute | solution.py:535
  234.9 18.8 %collective-permute-done.29.refs_2_ = bf16[2,160,960]{2,1,0:T(8,128)(2,1)S(1)} collective-permute-done((bf16[2,160,960]{2,1,0:T(8,128)(2,1)S(1)}, bf16[2,160,960]{2,1,0:T(8,128)(2,1)S(1)}, u32[]{:S(2)}, u32[]{:S(2)}) %collective-permute-start.29) | collective-permute-done | bytes 614432 | tf_op jit(solution)/shard_map/ppermute | solution.py:526
  257.9 9.2 %collective-permute-done.30.refs_3_.refs_7_.refs_8_ = bf16[2,1,1,1,32,2688]{5,4,3,2,1,0:T(8,128)(2,1)S(1)} collective-permute-done((bf16[2,1,1,1,32,2688]{5,4,3,2,1,0:T(8,128)(2,1)S(1)}, bf16[2,1,1,1,32,2688]{5,4,3,2,1,0:T(8,128)(2,1)S(1)}, u32[]{:S(2)}, u32[]{:S(2)}) %collective-permute-start.30) | collective-permute-done | bytes 344096 | tf_op jit(solution)/shard_map/ppermute | solution.py:526
  269.4 2.0 shard_map.330.refs_10_.mine_ref
  272.9 5.9 %collective-permute-done.37.other_ref = bf16[2,2,2,16,1280]{4,3,2,1,0:T(8,128)(2,1)} collective-permute-done((bf16[2,2,2,16,1280]{4,3,2,1,0:T(8,128)(2,1)}, bf16[2,2,2,16,1280]{4,3,2,1,0:T(8,128)(2,1)}, u32[]{:S(2)}, u32[]{:S(2)}) %collective-permute-start.37) | collective-permute-done | bytes 327712 | tf_op jit(solution)/shard_map/ppermute | solution.py:535
  285.0 2.6 shard_map.332
  287.6 1.9 collective-permute-done.36.refs_1_
  290.6 1.9 shard_map.333.refs_0_
  293.5 1.9 shard_map.334
  (197 shorter events, 53.9 us)
Async XLA Ops:
  7.2 119.1 %all-gather.2.cloned.1.call-start = ((), (), s32[]{:S(2)}) async-start(), calls=%async_computation | async-start | bytes 18104320 | tf_op jit(solution)/shard_map/all_gather | solution.py:582
  11.8 26.2 %collective-permute-start.3 = (bf16[512,1024]{1,0:T(8,128)(2,1)S(1)}, bf16[512,1024]{1,0:T(8,128)(2,1)}, u32[]{:S(2)}, u32[]{:S(2)}) collective-permute-start(bf16[512,1024]{1,0:T(8,128)(2,1)S(1)} %shard_map.312.cot_ref), channel_id=1, source_target_pairs={{0,1},{1,0},{2,3},{3,2},{4,5},{5,4},{6,7},{7,6},{8,9},{9,8},{10,11... | collective-permute-start | bytes 3145736 | tf_op jit(solution)/shard_map/ppermute | solution.py:526
  12.3 13.8 %collective-permute-start.2 = (bf16[2,16,2688]{2,1,0:T(8,128)(2,1)S(1)}, bf16[2,16,2688]{2,1,0:T(8,128)(2,1)S(1)}, u32[]{:S(2)}, u32[]{:S(2)}) collective-permute-start(bf16[2,16,2688]{2,1,0:T(8,128)(2,1)S(1)} %copy-done.35), channel_id=1, source_target_pairs={{0,12},{1,13},{2,14},{3,15},{4,8},{5,9},{6,10},{7,11},{8,4},{9,5},... | collective-permute-start | bytes 516104 | tf_op jit(solution)/shard_map/ppermute | solution.py:526
  17.0 13.7 %collective-permute-start.1 = (bf16[2,16,2688]{2,1,0:T(8,128)(2,1)S(1)}, bf16[2,16,2688]{2,1,0:T(8,128)(2,1)}, u32[]{:S(2)}, u32[]{:S(2)}) collective-permute-start(bf16[2,16,2688]{2,1,0:T(8,128)(2,1)S(1)} %copy-done.35), channel_id=1, source_target_pairs={{0,4},{1,5},{2,6},{3,7},{4,0},{5,1},{6,2},{7,3},{8,12},{9,13},{10,... | collective-permute-start | bytes 516104 | tf_op jit(solution)/shard_map/ppermute | solution.py:526
  17.0 21.0 %collective-permute-start = (bf16[2,16,2688]{2,1,0:T(8,128)(2,1)S(1)}, bf16[2,16,2688]{2,1,0:T(8,128)(2,1)}, u32[]{:S(2)}, u32[]{:S(2)}) collective-permute-start(bf16[2,16,2688]{2,1,0:T(8,128)(2,1)S(1)} %copy-done.35), channel_id=1, source_target_pairs={{0,8},{1,9},{2,10},{3,11},{4,12},{5,13},{6,14},{7,15},{8,0},{9,1},... | collective-permute-start | bytes 516104 | tf_op jit(solution)/shard_map/ppermute | solution.py:526
  40.9 32.2 %collective-permute-start.4 = (bf16[2,64,2688]{2,1,0:T(8,128)(2,1)S(1)}, bf16[2,64,2688]{2,1,0:T(8,128)(2,1)S(1)}, u32[]{:S(2)}, u32[]{:S(2)}) collective-permute-start(bf16[2,64,2688]{2,1,0:T(8,128)(2,1)S(1)} %shard_map.314.refs_0_), channel_id=1, source_target_pairs={{0,2},{1,3},{2,0},{3,1},{4,6},{5,7},{6,4},{7,5},{8,10},{9,11},{10,... | collective-permute-start | bytes 2064392 | tf_op jit(solution)/shard_map/ppermute | solution.py:526
  42.5 32.7 %collective-permute-start.5 = (bf16[2,64,2688]{2,1,0:T(8,128)(2,1)S(1)}, bf16[2,64,2688]{2,1,0:T(8,128)(2,1)S(1)}, u32[]{:S(2)}, u32[]{:S(2)}) collective-permute-start(bf16[2,64,2688]{2,1,0:T(8,128)(2,1)S(1)} %shard_map.314.refs_0_), channel_id=1, source_target_pairs={{0,16},{16,0},{1,17},{17,1},{2,18},{18,2},{3,19},{19,3},{4,20},{20... | collective-permute-start | bytes 2064392 | tf_op jit(solution)/shard_map/ppermute | solution.py:535
  73.1 15.0 %collective-permute-start.6 = (bf16[2,64,2688]{2,1,0:T(8,128)(2,1)S(1)}, bf16[2,64,2688]{2,1,0:T(8,128)(2,1)S(1)}, u32[]{:S(2)}, u32[]{:S(2)}) collective-permute-start(bf16[2,64,2688]{2,1,0:T(8,128)(2,1)S(1)} %collective-permute-done.4.refs_1_), channel_id=1, source_target_pairs={{0,16},{16,0},{1,17},{17,1},{2,18},{18,2},{3,19},{19,3},{4,20},{20... | collective-permute-start | bytes 2064392 | tf_op jit(solution)/shard_map/ppermute | solution.py:535
  74.6 13.5 %collective-permute-start.7 = (bf16[2,64,2688]{2,1,0:T(8,128)(2,1)S(1)}, bf16[2,64,2688]{2,1,0:T(8,128)(2,1)S(1)}, u32[]{:S(2)}, u32[]{:S(2)}) collective-permute-start(bf16[2,64,2688]{2,1,0:T(8,128)(2,1)S(1)} %shard_map.314.refs_0_), channel_id=1, source_target_pairs={{0,1},{1,0},{2,3},{3,2},{4,5},{5,4},{6,7},{7,6},{8,9},{9,8},{10,11... | collective-permute-start | bytes 2064392 | tf_op jit(solution)/shard_map/ppermute | solution.py:526
  74.6 13.5 %collective-permute-start.8 = (bf16[2,64,2688]{2,1,0:T(8,128)(2,1)S(1)}, bf16[2,64,2688]{2,1,0:T(8,128)(2,1)S(1)}, u32[]{:S(2)}, u32[]{:S(2)}) collective-permute-start(bf16[2,64,2688]{2,1,0:T(8,128)(2,1)S(1)} %collective-permute-done.4.refs_1_), channel_id=1, source_target_pairs={{0,1},{1,0},{2,3},{3,2},{4,5},{5,4},{6,7},{7,6},{8,9},{9,8},{10,11... | collective-permute-start | bytes 2064392 | tf_op jit(solution)/shard_map/ppermute | solution.py:526
  75.1 13.0 %collective-permute-start.9 = (bf16[2,64,2688]{2,1,0:T(8,128)(2,1)S(1)}, bf16[2,64,2688]{2,1,0:T(8,128)(2,1)S(1)}, u32[]{:S(2)}, u32[]{:S(2)}) collective-permute-start(bf16[2,64,2688]{2,1,0:T(8,128)(2,1)S(1)} %collective-permute-done.5.refs_2_), channel_id=1, source_target_pairs={{0,1},{1,0},{2,3},{3,2},{4,5},{5,4},{6,7},{7,6},{8,9},{9,8},{10,11... | collective-permute-start | bytes 2064392 | tf_op jit(solution)/shard_map/ppermute | solution.py:526
  161.8 30.3 %collective-permute-start.14 = (bf16[1024,512]{1,0:T(8,128)(2,1)}, bf16[1024,512]{1,0:T(8,128)(2,1)S(1)}, u32[]{:S(2)}, u32[]{:S(2)}) collective-permute-start(bf16[1024,512]{1,0:T(8,128)(2,1)} %get-tuple-element.67), channel_id=1, source_target_pairs={{0,1},{1,0},{2,3},{3,2},{4,5},{5,4},{6,7},{7,6},{8,9},{9,8},{10,11... | collective-permute-start | bytes 3145736 | tf_op jit(solution)/shard_map/ppermute | solution.py:526
  162.2 30.0 %collective-permute-start.13 = (bf16[512,1024]{1,0:T(8,128)(2,1)}, bf16[512,1024]{1,0:T(8,128)(2,1)S(1)}, u32[]{:S(2)}, u32[]{:S(2)}) collective-permute-start(bf16[512,1024]{1,0:T(8,128)(2,1)} %get-tuple-element.65), channel_id=1, source_target_pairs={{0,1},{1,0},{2,3},{3,2},{4,5},{5,4},{6,7},{7,6},{8,9},{9,8},{10,11... | collective-permute-start | bytes 3145736 | tf_op jit(solution)/shard_map/ppermute | solution.py:526
  162.3 31.3 %collective-permute-start.20 = (bf16[4,160,960]{2,1,0:T(8,128)(2,1)}, bf16[4,160,960]{2,1,0:T(8,128)(2,1)S(1)}, u32[]{:S(2)}, u32[]{:S(2)}) collective-permute-start(bf16[4,160,960]{2,1,0:T(8,128)(2,1)} %get-tuple-element.79), channel_id=1, source_target_pairs={{0,4},{1,5},{2,6},{3,7},{4,0},{5,1},{6,2},{7,3},{8,12},{9,13},{10,... | collective-permute-start | bytes 3686408 | tf_op jit(solution)/shard_map/ppermute | solution.py:526
  162.3 31.3 %collective-permute-start.21 = (bf16[2,2,2,64,1280]{4,3,2,1,0:T(8,128)(2,1)}, bf16[2,2,2,64,1280]{4,3,2,1,0:T(8,128)(2,1)S(1)}, u32[]{:S(2)}, u32[]{:S(2)}) collective-permute-start(bf16[2,2,2,64,1280]{4,3,2,1,0:T(8,128)(2,1)} %bitcast.53), channel_id=1, source_target_pairs={{0,16},{16,0},{1,17},{17,1},{2,18},{18,2},{3,19},{19,3},{4,20},{20... | collective-permute-start | bytes 3932168 | tf_op jit(solution)/shard_map/ppermute | solution.py:535
  164.5 31.1 %collective-permute-start.22 = (bf16[2,2,2,64,1280]{4,3,2,1,0:T(8,128)(2,1)}, bf16[2,2,2,64,1280]{4,3,2,1,0:T(8,128)(2,1)S(1)}, u32[]{:S(2)}, u32[]{:S(2)}) collective-permute-start(bf16[2,2,2,64,1280]{4,3,2,1,0:T(8,128)(2,1)} %bitcast.52), channel_id=1, source_target_pairs={{0,2},{1,3},{2,0},{3,1},{4,6},{5,7},{6,4},{7,5},{8,10},{9,11},{10,... | collective-permute-start | bytes 3932168 | tf_op jit(solution)/shard_map/ppermute | solution.py:526
  192.1 9.0 %collective-permute-start.18 = (bf16[512,1024]{1,0:T(8,128)(2,1)S(1)}, bf16[512,1024]{1,0:T(8,128)(2,1)S(1)}, u32[]{:S(2)}, u32[]{:S(2)}) collective-permute-start(bf16[512,1024]{1,0:T(8,128)(2,1)S(1)} %get-tuple-element.76.refs_2_), channel_id=1, source_target_pairs={{0,1},{1,0},{2,3},{3,2},{4,5},{5,4},{6,7},{7,6},{8,9},{9,8},{10,11... | collective-permute-start | bytes 3145736 | tf_op jit(solution)/shard_map/ppermute | solution.py:526
  192.2 8.9 %collective-permute-start.16 = (bf16[512,1024]{1,0:T(8,128)(2,1)S(1)}, bf16[512,1024]{1,0:T(8,128)(2,1)S(1)}, u32[]{:S(2)}, u32[]{:S(2)}) collective-permute-start(bf16[512,1024]{1,0:T(8,128)(2,1)S(1)} %get-tuple-element.74.refs_2_.refs_0_), channel_id=1, source_target_pairs={{0,1},{1,0},{2,3},{3,2},{4,5},{5,4},{6,7},{7,6},{8,9},{9,8},{10,11... | collective-permute-start | bytes 3145736 | tf_op jit(solution)/shard_map/ppermute | solution.py:526
  197.7 17.9 %collective-permute-start.25 = (bf16[2,2,1,64,1280]{4,3,2,1,0:T(8,128)(2,1)}, bf16[2,2,1,64,1280]{4,3,2,1,0:T(8,128)(2,1)}, u32[]{:S(2)}, u32[]{:S(2)}) collective-permute-start(bf16[2,2,1,64,1280]{4,3,2,1,0:T(8,128)(2,1)} %get-tuple-element.84.refs_10_), channel_id=1, source_target_pairs={{0,2},{1,3},{2,0},{3,1},{4,6},{5,7},{6,4},{7,5},{8,10},{9,11},{10,... | collective-permute-start | bytes 1966088 | tf_op jit(solution)/shard_map/ppermute | solution.py:526
  199.5 17.9 %collective-permute-start.26 = (bf16[2,2,1,64,1280]{4,3,2,1,0:T(8,128)(2,1)}, bf16[2,2,1,64,1280]{4,3,2,1,0:T(8,128)(2,1)}, u32[]{:S(2)}, u32[]{:S(2)}) collective-permute-start(bf16[2,2,1,64,1280]{4,3,2,1,0:T(8,128)(2,1)} %get-tuple-element.85.refs_11_), channel_id=1, source_target_pairs={{0,16},{16,0},{1,17},{17,1},{2,18},{18,2},{3,19},{19,3},{4,20},{20... | collective-permute-start | bytes 1966088 | tf_op jit(solution)/shard_map/ppermute | solution.py:535
  206.4 25.1 %collective-permute-start.23 = (bf16[1,1,2,64,2688]{4,3,2,1,0:T(8,128)(2,1)}, bf16[1,1,2,64,2688]{4,3,2,1,0:T(8,128)(2,1)}, u32[]{:S(2)}, u32[]{:S(2)}) collective-permute-start(bf16[1,1,2,64,2688]{4,3,2,1,0:T(8,128)(2,1)} %bitcast.17), channel_id=1, source_target_pairs={{0,16},{16,0},{1,17},{17,1},{2,18},{18,2},{3,19},{19,3},{4,20},{20... | collective-permute-start | bytes 2064392 | tf_op jit(solution)/shard_map/ppermute | solution.py:535
  206.9 24.6 %collective-permute-start.24 = (bf16[1,1,2,64,2688]{4,3,2,1,0:T(8,128)(2,1)}, bf16[1,1,2,64,2688]{4,3,2,1,0:T(8,128)(2,1)}, u32[]{:S(2)}, u32[]{:S(2)}) collective-permute-start(bf16[1,1,2,64,2688]{4,3,2,1,0:T(8,128)(2,1)} %bitcast.19), channel_id=1, source_target_pairs={{0,2},{1,3},{2,0},{3,1},{4,6},{5,7},{6,4},{7,5},{8,10},{9,11},{10,... | collective-permute-start | bytes 2064392 | tf_op jit(solution)/shard_map/ppermute | solution.py:526
  222.7 32.5 %collective-permute-start.31 = (bf16[2,2,2,1,32,1280]{5,4,3,2,1,0:T(8,128)(2,1)S(1)}, bf16[2,2,2,1,32,1280]{5,4,3,2,1,0:T(8,128)(2,1)S(1)}, u32[]{:S(2)}, u32[]{:S(2)}) collective-permute-start(bf16[2,2,2,1,32,1280]{5,4,3,2,1,0:T(8,128)(2,1)S(1)} %shard_map.323.refs_4_), channel_id=1, source_target_pairs={{0,4},{1,5},{2,6},{3,7},{4,0},{5,1},{6,2},{7,3},{8,12},{9,13},{10,... | collective-permute-start | bytes 1966088 | tf_op jit(solution)/shard_map/ppermute | solution.py:526
  224.6 29.1 %collective-permute-start.29 = (bf16[2,160,960]{2,1,0:T(8,128)(2,1)S(1)}, bf16[2,160,960]{2,1,0:T(8,128)(2,1)S(1)}, u32[]{:S(2)}, u32[]{:S(2)}) collective-permute-start(bf16[2,160,960]{2,1,0:T(8,128)(2,1)S(1)} %copy-done.23), channel_id=1, source_target_pairs={{0,8},{1,9},{2,10},{3,11},{4,12},{5,13},{6,14},{7,15},{8,0},{9,1},... | collective-permute-start | bytes 1843208 | tf_op jit(solution)/shard_map/ppermute | solution.py:526
  232.9 20.9 %collective-permute-start.27 = (bf16[1,1,1,64,2688]{4,3,2,1,0:T(8,128)(2,1)S(1)}, bf16[1,1,1,64,2688]{4,3,2,1,0:T(8,128)(2,1)S(1)}, u32[]{:S(2)}, u32[]{:S(2)}) collective-permute-start(bf16[1,1,1,64,2688]{4,3,2,1,0:T(8,128)(2,1)S(1)} %get-tuple-element.91.refs_3_), channel_id=1, source_target_pairs={{0,2},{1,3},{2,0},{3,1},{4,6},{5,7},{6,4},{7,5},{8,10},{9,11},{10,... | collective-permute-start | bytes 1032200 | tf_op jit(solution)/shard_map/ppermute | solution.py:526
  233.3 20.5 %collective-permute-start.28 = (bf16[1,1,1,64,2688]{4,3,2,1,0:T(8,128)(2,1)S(1)}, bf16[1,1,1,64,2688]{4,3,2,1,0:T(8,128)(2,1)S(1)}, u32[]{:S(2)}, u32[]{:S(2)}) collective-permute-start(bf16[1,1,1,64,2688]{4,3,2,1,0:T(8,128)(2,1)S(1)} %get-tuple-element.92.refs_4_), channel_id=1, source_target_pairs={{0,16},{16,0},{1,17},{17,1},{2,18},{18,2},{3,19},{19,3},{4,20},{20... | collective-permute-start | bytes 1032200 | tf_op jit(solution)/shard_map/ppermute | solution.py:535
  255.1 12.0 %collective-permute-start.30 = (bf16[2,1,1,1,32,2688]{5,4,3,2,1,0:T(8,128)(2,1)S(1)}, bf16[2,1,1,1,32,2688]{5,4,3,2,1,0:T(8,128)(2,1)S(1)}, u32[]{:S(2)}, u32[]{:S(2)}) collective-permute-start(bf16[2,1,1,1,32,2688]{5,4,3,2,1,0:T(8,128)(2,1)S(1)} %shard_map.326.refs_8_), channel_id=1, source_target_pairs={{0,4},{1,5},{2,6},{3,7},{4,0},{5,1},{6,2},{7,3},{8,12},{9,13},{10,... | collective-permute-start | bytes 1032200 | tf_op jit(solution)/shard_map/ppermute | solution.py:526
  256.9 12.6 %collective-permute-start.33 = (bf16[2,2,2,1,16,1280]{5,4,3,2,1,0:T(8,128)(2,1)S(1)}, bf16[2,2,2,1,16,1280]{5,4,3,2,1,0:T(8,128)(2,1)S(1)}, u32[]{:S(2)}, u32[]{:S(2)}) collective-permute-start(bf16[2,2,2,1,16,1280]{5,4,3,2,1,0:T(8,128)(2,1)S(1)} %shard_map.327.refs_8_), channel_id=1, source_target_pairs={{0,8},{1,9},{2,10},{3,11},{4,12},{5,13},{6,14},{7,15},{8,0},{9,1},... | collective-permute-start | bytes 983048 | tf_op jit(solution)/shard_map/ppermute | solution.py:526
  257.9 10.2 %collective-permute-start.34 = (bf16[1,160,960]{2,1,0:T(8,128)(2,1)S(1)}, bf16[1,160,960]{2,1,0:T(8,128)(2,1)S(1)}, u32[]{:S(2)}, u32[]{:S(2)}) collective-permute-start(bf16[1,160,960]{2,1,0:T(8,128)(2,1)S(1)} %shard_map.325.refs_6_), channel_id=1, source_target_pairs={{0,2},{1,3},{2,0},{3,1},{4,6},{5,7},{6,4},{7,5},{8,10},{9,11},{10,... | collective-permute-start | bytes 921608 | tf_op jit(solution)/shard_map/ppermute | solution.py:526
  272.9 12.1 %collective-permute-start.38 = (bf16[2,2,2,16,1280]{4,3,2,1,0:T(8,128)(2,1)}, bf16[2,2,2,16,1280]{4,3,2,1,0:T(8,128)(2,1)}, u32[]{:S(2)}, u32[]{:S(2)}) collective-permute-start(bf16[2,2,2,16,1280]{4,3,2,1,0:T(8,128)(2,1)} %shard_map.330.refs_10_.mine_ref), channel_id=1, source_target_pairs={{0,1},{1,0},{2,3},{3,2},{4,5},{5,4},{6,7},{7,6},{8,9},{9,8},{10,11... | collective-permute-start | bytes 983048 | tf_op jit(solution)/shard_map/ppermute | solution.py:526
  278.8 10.7 %collective-permute-start.36 = (bf16[1,160,960]{2,1,0:T(8,128)(2,1)}, bf16[1,160,960]{2,1,0:T(8,128)(2,1)S(1)}, u32[]{:S(2)}, u32[]{:S(2)}) collective-permute-start(bf16[1,160,960]{2,1,0:T(8,128)(2,1)} %shard_map.329.refs_10_.refs_0_), channel_id=1, source_target_pairs={{0,16},{16,0},{1,17},{17,1},{2,18},{18,2},{3,19},{19,3},{4,20},{20... | collective-permute-start | bytes 921608 | tf_op jit(solution)/shard_map/ppermute | solution.py:535
  281.8 11.0 %collective-permute-start.35 = (bf16[1,1,2,16,2688]{4,3,2,1,0:T(8,128)(2,1)S(1)}, bf16[1,1,2,16,2688]{4,3,2,1,0:T(8,128)(2,1)S(1)}, u32[]{:S(2)}, u32[]{:S(2)}) collective-permute-start(bf16[1,1,2,16,2688]{4,3,2,1,0:T(8,128)(2,1)S(1)} %shard_map.331.mine_ref), channel_id=1, source_target_pairs={{0,16},{16,0},{1,17},{17,1},{2,18},{18,2},{3,19},{19,3},{4,20},{20... | collective-permute-start | bytes 516104 | tf_op jit(solution)/shard_map/ppermute | solution.py:535
  (66 other events, 543.3 us)
Sparse Core Ops, SparseCore 0:
  10.9 109.1 all-gather.1
